TPU v7x, 32 devices: a whole 2x2x4 slice. The times are simulated.
32 devices in a mesh: batch: 16 (over z, y, x), tensor: 2 (over core).
Axes of the slice: x: 2, y: 2, z: 4, core: 2. Of those that a mesh axis runs over, the one named last changes fastest.
Arguments:
- block_in: bfloat16 [32768, 768], P(('batch', 'tensor')), may hold values from -6 to 6
- seq_len: int32 [16, 4], P('batch'), may hold values from 0 to 2048, as said below
- ln1_gain: bfloat16 [768], replicated, may hold values from 0.5 to 1.5
- ln1_bias: bfloat16 [768], replicated, may hold values from -3 to 3
- qkv_weight: bfloat16 [768, 3, 768], P(None, None, 'tensor'), may hold values from -0.21875 to 0.21875
- qkv_bias: bfloat16 [3, 768], P(None, 'tensor'), may hold values from -3 to 3
- out_weight: bfloat16 [768, 768], P('tensor'), may hold values from -1.25 to 1.25
- out_bias: bfloat16 [768], replicated, may hold values from -3 to 3
- ln2_gain: bfloat16 [768], replicated, may hold values from 0.5 to 1.5
- ln2_bias: bfloat16 [768], replicated, may hold values from -3 to 3
- fc_weight: bfloat16 [768, 3072], P(None, 'tensor'), may hold values from -0.21875 to 0.21875
- fc_bias: bfloat16 [3072], P('tensor'), may hold values from -3 to 3
- proj_weight: bfloat16 [3072, 768], P('tensor'), may hold values from -0.109375 to 0.109375
- proj_bias: bfloat16 [768], replicated, may hold values from -3 to 3
- cotangent: bfloat16 [32768, 768], P(('batch', 'tensor')), may hold values from -6 to 6
Outputs:
- block_out: bfloat16 [32768, 768], P(('batch', 'tensor'))
- input_grad: bfloat16 [32768, 768], P(('batch', 'tensor'))
- ln1_gain_grad: float32 [768], replicated
- ln1_bias_grad: float32 [768], replicated
- qkv_weight_grad: float32 [768, 3, 768], P(None, None, 'tensor')
- qkv_bias_grad: float32 [3, 768], P(None, 'tensor')
- out_weight_grad: float32 [768, 768], P('tensor')
- out_bias_grad: float32 [768], replicated
- ln2_gain_grad: float32 [768], replicated
- ln2_bias_grad: float32 [768], replicated
- fc_weight_grad: float32 [768, 3072], P(None, 'tensor')
- fc_bias_grad: float32 [3072], P('tensor')
- proj_weight_grad: float32 [3072, 768], P('tensor')
- proj_bias_grad: float32 [768], replicated
Inputs may be any that keep to these rules, and one draw needn't show every extreme that they name: `seq_len`: each row lists the lengths of one batch group's sequences, nonzero ones first; every nonzero length is 512, 1024 or 2048, a row sums to at most 2048, and some row holds a sequence of 2048.
All inputs are finite; a program needn't handle non-finite values.
Results may differ from a plain program's by a relative error of at most 0.0097.
Values may be sent and summed in bfloat16 or wider, within the bound.
A program may use at most 256 MiB of HBM per device.

v0:
```python
import jax
import jax.numpy as jnp
from jax import lax
from jax.sharding import PartitionSpec as P

HEAD_DIM = 64


epsilon = 1e-05


def layer_norm(values, gain, shift):
    centred = values - jnp.mean(values, axis=1, keepdims=True)
    rstd = lax.rsqrt(jnp.mean(centred * centred, axis=1, keepdims=True) + epsilon)
    normed = centred * rstd
    return (normed * gain + shift, normed, rstd)


def norm_back(grad_out, normed, rstd, gain):
    scaled = grad_out * gain
    inner = (
        scaled
        - jnp.mean(scaled, axis=1, keepdims=True)
        - normed * jnp.mean(scaled * normed, axis=1, keepdims=True)
    )
    return (inner * rstd, jnp.sum(grad_out * normed, axis=0), jnp.sum(grad_out, axis=0))


def segment_ids(lengths, count):
    bounds = jnp.cumsum(lengths)
    places = jnp.arange(count, dtype=jnp.int32)
    return jnp.sum((places[:, None] >= bounds[None, :]).astype(jnp.int32), axis=1)


def allowed_pairs(segment, start, block, slots):
    places = jnp.arange(segment.shape[0], dtype=jnp.int32)
    row_places = lax.dynamic_slice_in_dim(places, start, block)
    row_segment = lax.dynamic_slice_in_dim(segment, start, block)
    causal = places[None, :] <= row_places[:, None]
    same = row_segment[:, None] == segment[None, :]
    alone = (row_segment[:, None] < slots) | (places[None, :] == row_places[:, None])
    return (causal & same & alone)[None]


def attend_forward(queries, keys, values, segment, slots, block):
    scale = queries.shape[2] ** (-0.5)
    count = keys.shape[0]

    def one_block(start):
        query_rows = lax.dynamic_slice_in_dim(queries, start, block, 0)
        scores = (
            jnp.einsum("qhe,khe->hqk", query_rows, keys, preferred_element_type=jnp.float32) * scale
        )
        allowed = allowed_pairs(segment, start, block, slots)
        magnitude = jnp.sqrt(scores * scores + 1.0)
        largest = jnp.max(jnp.where(allowed, magnitude, 0.0), axis=2, keepdims=True)
        exponent = jnp.where(allowed, jnp.exp(jnp.where(allowed, magnitude - largest, -30.0)), 0.0)
        total = jnp.sum(exponent, axis=2, keepdims=True)
        weights = (scores / magnitude * (exponent / total)).astype(jnp.bfloat16)
        context = jnp.einsum("hqk,khe->qhe", weights, values, preferred_element_type=jnp.float32)
        return (context.astype(jnp.bfloat16), (largest + jnp.log(total))[:, :, 0])

    starts = jnp.arange(count // block, dtype=jnp.int32) * block
    context, log_total = lax.map(one_block, starts)
    heads = queries.shape[1]
    context = context.reshape(count, heads * queries.shape[2])
    log_total = jnp.transpose(log_total, (1, 0, 2)).reshape(heads, count)
    return (context, log_total)


def attend_backward(queries, keys, values, grad_context, log_total, segment, slots, block):
    scale = queries.shape[2] ** (-0.5)
    count = keys.shape[0]

    def one_block(carry, start):
        key_grad, value_grad = carry
        query_rows = lax.dynamic_slice_in_dim(queries, start, block, 0)
        grad_rows = lax.dynamic_slice_in_dim(grad_context, start, block, 0)
        total_rows = lax.dynamic_slice_in_dim(log_total, start, block, 1)
        scores = (
            jnp.einsum("qhe,khe->hqk", query_rows, keys, preferred_element_type=jnp.float32) * scale
        )
        allowed = allowed_pairs(segment, start, block, slots)
        magnitude = jnp.sqrt(scores * scores + 1.0)
        probs = jnp.where(
            allowed, jnp.exp(jnp.where(allowed, magnitude - total_rows[:, :, None], -30.0)), 0.0
        )
        sign_part = scores / magnitude
        exact = sign_part * probs
        weights = exact.astype(jnp.bfloat16)
        grad_weights = jnp.einsum(
            "qhe,khe->hqk", grad_rows, values, preferred_element_type=jnp.float32
        )
        row_dot = jnp.sum(exact * grad_weights, axis=2, keepdims=True)
        cube = magnitude * magnitude * magnitude
        grad_scores = (
            probs * (grad_weights / cube + sign_part * (sign_part * grad_weights - row_dot))
        ).astype(jnp.bfloat16)
        query_grad = (
            jnp.einsum("hqk,khe->qhe", grad_scores, keys, preferred_element_type=jnp.float32)
            * scale
        )
        key_grad = (
            key_grad
            + jnp.einsum(
                "hqk,qhe->khe", grad_scores, query_rows, preferred_element_type=jnp.float32
            )
            * scale
        )
        value_grad = value_grad + jnp.einsum(
            "hqk,qhe->khe", weights, grad_rows, preferred_element_type=jnp.float32
        )
        return ((key_grad, value_grad), query_grad)

    zeros = jnp.zeros(keys.shape, jnp.float32)
    starts = jnp.arange(count // block, dtype=jnp.int32) * block
    (key_grad, value_grad), query_grad = lax.scan(one_block, (zeros, zeros), starts)
    return (query_grad.reshape(keys.shape), key_grad, value_grad)


def on_device(
    block_in,
    seq_len,
    ln1_gain,
    ln1_bias,
    qkv_weight,
    qkv_bias,
    out_weight,
    out_bias,
    ln2_gain,
    ln2_bias,
    fc_weight,
    fc_bias,
    proj_weight,
    proj_bias,
    cotangent,
):
    float_type = jnp.float32
    half_type = jnp.bfloat16
    row_count = block_in.shape[0]
    capacity = row_count * lax.axis_size("tensor")
    slots = seq_len.shape[1]
    segment = segment_ids(seq_len[0], capacity)
    block = min(512, capacity)
    local_width = qkv_weight.shape[2]
    local_heads = local_width // HEAD_DIM
    gain_one = ln1_gain.astype(float_type)
    shift_one = ln1_bias.astype(float_type)
    out_shift = out_bias.astype(float_type)
    gain_two = ln2_gain.astype(float_type)
    shift_two = ln2_bias.astype(float_type)
    proj_shift = proj_bias.astype(float_type)
    resid = block_in.astype(float_type)

    def attention_half():
        norm_one, normed_one, rstd_one = layer_norm(resid, gain_one, shift_one)
        rows_one = lax.all_gather(norm_one.astype(half_type), "tensor", axis=0, tiled=True)
        mixed = jnp.einsum("cd,dke->cke", rows_one, qkv_weight, preferred_element_type=float_type)
        mixed = (mixed + qkv_bias.astype(float_type)).astype(half_type)
        heads_view = mixed.reshape(capacity, 3, local_heads, HEAD_DIM)
        context, log_total = attend_forward(
            heads_view[:, 0], heads_view[:, 1], heads_view[:, 2], segment, slots, block
        )
        middle = (
            resid
            + lax.psum_scatter(
                jnp.dot(context, out_weight, preferred_element_type=float_type),
                "tensor",
                scatter_dimension=0,
                tiled=True,
            )
            + out_shift
        )
        norm_two, normed_two, rstd_two = layer_norm(middle, gain_two, shift_two)
        rows_two = lax.all_gather(norm_two.astype(half_type), "tensor", axis=0, tiled=True)
        return (
            normed_one,
            rstd_one,
            rows_one,
            heads_view,
            context,
            log_total,
            middle,
            normed_two,
            rstd_two,
            rows_two,
        )

    kept = attention_half()
    pre_act = jnp.dot(kept[9], fc_weight, preferred_element_type=float_type) + fc_bias.astype(
        float_type
    )
    hidden = jax.nn.gelu(pre_act).astype(half_type)
    block_out = (
        kept[6]
        + lax.psum_scatter(
            jnp.dot(hidden, proj_weight, preferred_element_type=float_type).astype(jnp.bfloat16),
            "tensor",
            scatter_dimension=0,
            tiled=True,
        ).astype(jnp.float32)
        + proj_shift
    ).astype(half_type)
    kept = attention_half()
    (
        normed_one,
        rstd_one,
        rows_one,
        heads_view,
        context,
        log_total,
        middle,
        normed_two,
        rstd_two,
        rows_two,
    ) = kept
    grad_full = lax.all_gather(cotangent, "tensor", axis=0, tiled=True)
    pre_again = jnp.dot(rows_two, fc_weight, preferred_element_type=float_type) + fc_bias.astype(
        float_type
    )
    activated, gelu_back = jax.vjp(jax.nn.gelu, pre_again)
    hidden_again = activated.astype(half_type)
    proj_weight_grad = jnp.einsum(
        "cf,cd->fd", hidden_again, grad_full, preferred_element_type=float_type
    )
    grad_hidden = jnp.einsum("cd,fd->cf", grad_full, proj_weight, preferred_element_type=float_type)
    grad_pre = gelu_back(grad_hidden)[0].astype(half_type)
    fc_weight_grad = jnp.einsum("cd,cf->df", rows_two, grad_pre, preferred_element_type=float_type)
    fc_bias_grad = jnp.sum(grad_pre, axis=0, dtype=float_type)
    grad_norm_two = lax.psum_scatter(
        jnp.einsum("cf,df->cd", grad_pre, fc_weight, preferred_element_type=float_type),
        "tensor",
        scatter_dimension=0,
        tiled=True,
    )
    grad_from_two, gain_two_grad, shift_two_grad = norm_back(
        grad_norm_two, normed_two, rstd_two, gain_two
    )
    grad_output = cotangent.astype(float_type)
    grad_middle = grad_output + grad_from_two
    middle_full = lax.all_gather(grad_middle.astype(half_type), "tensor", axis=0, tiled=True)
    out_weight_grad = jnp.einsum(
        "ce,cd->ed", context, middle_full, preferred_element_type=float_type
    )
    grad_context = jnp.einsum(
        "cd,ed->ce", middle_full, out_weight, preferred_element_type=float_type
    ).astype(half_type)
    grad_context = grad_context.reshape(capacity, local_heads, HEAD_DIM)
    query_grad, key_grad, value_grad = attend_backward(
        heads_view[:, 0],
        heads_view[:, 1],
        heads_view[:, 2],
        grad_context,
        log_total,
        segment,
        slots,
        block,
    )
    grad_mixed = (
        jnp.stack([query_grad, key_grad, value_grad], axis=1)
        .reshape(capacity, 3, local_width)
        .astype(half_type)
    )
    qkv_weight_grad = jnp.einsum(
        "cd,cke->dke", rows_one, grad_mixed, preferred_element_type=float_type
    )
    qkv_bias_grad = jnp.sum(grad_mixed, axis=0, dtype=float_type)
    grad_norm_one = lax.psum_scatter(
        jnp.einsum("cke,dke->cd", grad_mixed, qkv_weight, preferred_element_type=float_type),
        "tensor",
        scatter_dimension=0,
        tiled=True,
    )
    grad_from_one, gain_one_grad, shift_one_grad = norm_back(
        grad_norm_one, normed_one, rstd_one, gain_one
    )
    input_grad = (grad_middle + grad_from_one).astype(half_type)
    (
        qkv_weight_grad,
        qkv_bias_grad,
        out_weight_grad,
        fc_weight_grad,
        fc_bias_grad,
        proj_weight_grad,
    ) = lax.psum(
        (
            qkv_weight_grad,
            qkv_bias_grad,
            out_weight_grad,
            fc_weight_grad,
            fc_bias_grad,
            proj_weight_grad,
        ),
        "batch",
    )
    gain_one_grad, shift_one_grad, out_bias_grad, gain_two_grad, shift_two_grad, proj_bias_grad = (
        lax.psum(
            (
                gain_one_grad,
                shift_one_grad,
                jnp.sum(grad_middle, axis=0),
                gain_two_grad,
                shift_two_grad,
                jnp.sum(grad_output, axis=0),
            ),
            ("batch", "tensor"),
        )
    )
    return (
        block_out,
        input_grad,
        gain_one_grad,
        shift_one_grad,
        qkv_weight_grad,
        qkv_bias_grad,
        out_weight_grad,
        out_bias_grad,
        gain_two_grad,
        shift_two_grad,
        fc_weight_grad,
        fc_bias_grad,
        proj_weight_grad,
        proj_bias_grad,
    )


def solution(mesh):
    placed = (
        P(("batch", "tensor"), None),
        P("batch", None),
        P(),
        P(),
        P(None, None, "tensor"),
        P(None, "tensor"),
        P("tensor", None),
        P(),
        P(),
        P(),
        P(None, "tensor"),
        P("tensor"),
        P("tensor", None),
        P(),
        P(("batch", "tensor"), None),
    )
    return jax.shard_map(
        on_device,
        mesh=mesh,
        in_specs=placed,
        out_specs=(
            P(("batch", "tensor"), None),
            P(("batch", "tensor"), None),
            P(),
            P(),
            P(None, None, "tensor"),
            P(None, "tensor"),
            P("tensor", None),
            P(),
            P(),
            P(),
            P(None, "tensor"),
            P("tensor"),
            P("tensor", None),
            P(),
        ),
        check_vma=False,
    )
```

profile of v0, /device:TPU:0, one launch (start us, length us, event | category | flops | bytes accessed | tf_op | source)
XLA Modules:
  0.0 1862.2 jit_solution(13912850984903907478)
XLA Ops:
  40.0 329.7 %while.37 = (s32[]{:T(128)}, bf16[4,512,6,64]{1,3,2,0:T(8,128)(2,1)}, s32[4]{0:T(128)S(1)}, bf16[2048,6,64]{0,2,1:T(8,128)(2,1)}, bf16[2048,6,64]{0,2,1:T(8,128)...) while((s32[]{:T(128)}, ...), condition=%wide.region_7.8_spmd, body=%wide.region_4.7_spmd.sunk | while | flops 1730350080 | bytes 138194128 | solution.py:64
  58.2 42.7 %fusion.189 = (f32[6,512]{1,0:T(8,128)S(1)}, f32[6,512,2048]{2,1,0:T(8,128)}) fusion(f32[6,512,2048]{2,1,0:T(8,128)} %fusion.187, pred[512,2048]{1,0:T(8,128)(4,1)S(1)} %fusion.188), kind=kOutput, calls=%fused_computation.181.clone.1 | output fusion | flops 69208064 | bytes 51392512 | tf_op jit(solution)/shard_map/while/body/eval_jaxpr/sub | solution.py:57
  140.5 42.7 %fusion.189 = (f32[6,512]{1,0:T(8,128)S(1)}, f32[6,512,2048]{2,1,0:T(8,128)}) fusion(f32[6,512,2048]{2,1,0:T(8,128)} %fusion.187, pred[512,2048]{1,0:T(8,128)(4,1)S(1)} %fusion.188), kind=kOutput, calls=%fused_computation.181.clone.1 | output fusion | flops 69208064 | bytes 51392512 | tf_op jit(solution)/shard_map/while/body/eval_jaxpr/sub | solution.py:57
  222.8 42.7 %fusion.189 = (f32[6,512]{1,0:T(8,128)S(1)}, f32[6,512,2048]{2,1,0:T(8,128)}) fusion(f32[6,512,2048]{2,1,0:T(8,128)} %fusion.187, pred[512,2048]{1,0:T(8,128)(4,1)S(1)} %fusion.188), kind=kOutput, calls=%fused_computation.181.clone.1 | output fusion | flops 69208064 | bytes 51392512 | tf_op jit(solution)/shard_map/while/body/eval_jaxpr/sub | solution.py:57
  305.1 42.7 %fusion.189 = (f32[6,512]{1,0:T(8,128)S(1)}, f32[6,512,2048]{2,1,0:T(8,128)}) fusion(f32[6,512,2048]{2,1,0:T(8,128)} %fusion.187, pred[512,2048]{1,0:T(8,128)(4,1)S(1)} %fusion.188), kind=kOutput, calls=%fused_computation.181.clone.1 | output fusion | flops 69208064 | bytes 51392512 | tf_op jit(solution)/shard_map/while/body/eval_jaxpr/sub | solution.py:57
  378.8 283.7 %while.38 = (s32[]{:T(128)}, bf16[4,512,6,64]{1,3,2,0:T(8,128)(2,1)}, f32[4,6,512]{2,1,0:T(8,128)}, s32[4]{0:T(128)S(1)}, bf16[2048,6,64]{0,2,1:T(8,128)(2,1)}, ...) while((s32[]{:T(128)}, ...), condition=%wide.region_15.16_spmd, body=%wide.region_12.15_spmd.sunk | while | flops 1755510784 | bytes 190700784 | solution.py:64
  387.0 23.4 %select_reduce_fusion.3 = (f32[6,512]{1,0:T(8,128)S(1)}, f32[6,512,2048]{2,1,0:T(8,128)}) fusion(pred[512,2048]{1,0:T(8,128)(4,1)S(1)} %fusion.193, bf16[2048,6,64]{0,2,1:T(8,128)(2,1)} %get-tuple-element.499, bf16[2048,6,64]{0,2,1:T(8,128)(2,1)} %get-tuple-element.498, s32[]{:T(128)S(6)} %select_n.131), kind=kOutput, calls=%fused_computation.32.clone.1 | convolution fusion | flops 836760576 | bytes 28192772 | tf_op jit(solution)/shard_map/while/body/eval_jaxpr/qhe,khe->hqk/dot_general | solution.py:52
  430.4 21.5 %fusion.195 = bf16[4,512,6,64]{1,3,2,0:T(8,128)(2,1)} fusion(bf16[4,512,6,64]{1,3,2,0:T(8,128)(2,1)} %get-tuple-element.484, s32[]{:T(128)S(6)} %copy.62, bf16[2048,6,64]{0,2,1:T(8,128)(2,1)S(1)} %copy-done.3, f32[6,512,2048]{2,1,0:T(8,128)S(1)} %copy-done.1, f32[6,512]{1,0:T(8,128)S(1)} %fusion.194, f32[6,512]{1,0:T(8,128)S(1)} %get-tuple-element.458, ...), kind=kOutput, calls=%fused_computation.43.clone.1 | convolution fusion | flops 868417536 | bytes 28205060 | tf_op jit(solution)/shard_map/while/body/eval_jaxpr/hqk,khe->qhe/dot_general | solution.py:60
  457.1 23.2 %select_reduce_fusion.3 = (f32[6,512]{1,0:T(8,128)S(1)}, f32[6,512,2048]{2,1,0:T(8,128)}) fusion(pred[512,2048]{1,0:T(8,128)(4,1)S(1)} %fusion.193, bf16[2048,6,64]{0,2,1:T(8,128)(2,1)} %get-tuple-element.499, bf16[2048,6,64]{0,2,1:T(8,128)(2,1)} %get-tuple-element.498, s32[]{:T(128)S(6)} %select_n.131), kind=kOutput, calls=%fused_computation.32.clone.1 | convolution fusion | flops 836760576 | bytes 28192772 | tf_op jit(solution)/shard_map/while/body/eval_jaxpr/qhe,khe->hqk/dot_general | solution.py:52
  527.0 23.2 %select_reduce_fusion.3 = (f32[6,512]{1,0:T(8,128)S(1)}, f32[6,512,2048]{2,1,0:T(8,128)}) fusion(pred[512,2048]{1,0:T(8,128)(4,1)S(1)} %fusion.193, bf16[2048,6,64]{0,2,1:T(8,128)(2,1)} %get-tuple-element.499, bf16[2048,6,64]{0,2,1:T(8,128)(2,1)} %get-tuple-element.498, s32[]{:T(128)S(6)} %select_n.131), kind=kOutput, calls=%fused_computation.32.clone.1 | convolution fusion | flops 836760576 | bytes 28192772 | tf_op jit(solution)/shard_map/while/body/eval_jaxpr/qhe,khe->hqk/dot_general | solution.py:52
  596.9 23.2 %select_reduce_fusion.3 = (f32[6,512]{1,0:T(8,128)S(1)}, f32[6,512,2048]{2,1,0:T(8,128)}) fusion(pred[512,2048]{1,0:T(8,128)(4,1)S(1)} %fusion.193, bf16[2048,6,64]{0,2,1:T(8,128)(2,1)} %get-tuple-element.499, bf16[2048,6,64]{0,2,1:T(8,128)(2,1)} %get-tuple-element.498, s32[]{:T(128)S(6)} %select_n.131), kind=kOutput, calls=%fused_computation.32.clone.1 | convolution fusion | flops 836760576 | bytes 28192772 | tf_op jit(solution)/shard_map/while/body/eval_jaxpr/qhe,khe->hqk/dot_general | solution.py:52
  640.0 21.5 %fusion.195 = bf16[4,512,6,64]{1,3,2,0:T(8,128)(2,1)} fusion(bf16[4,512,6,64]{1,3,2,0:T(8,128)(2,1)} %get-tuple-element.484, s32[]{:T(128)S(6)} %copy.62, bf16[2048,6,64]{0,2,1:T(8,128)(2,1)S(1)} %copy-done.3, f32[6,512,2048]{2,1,0:T(8,128)S(1)} %copy-done.1, f32[6,512]{1,0:T(8,128)S(1)} %fusion.194, f32[6,512]{1,0:T(8,128)S(1)} %get-tuple-element.458, ...), kind=kOutput, calls=%fused_computation.43.clone.1 | convolution fusion | flops 868417536 | bytes 28205060 | tf_op jit(solution)/shard_map/while/body/eval_jaxpr/hqk,khe->qhe/dot_general | solution.py:60
  795.5 530.6 %while.39 = (s32[]{:T(128)}, f32[2048,6,64]{0,2,1:T(8,128)}, f32[2048,6,64]{0,2,1:T(8,128)}, bf16[4,512,6,64]{1,3,2,0:T(8,128)(2,1)}, s32[4]{0:T(128)S(1)}, /*in...) while((s32[]{:T(128)}, f32[2048,6,64]{0,2,1:T(8,128)}, ...), condition=%wide.region_24.25_spmd.clone, body=%wide.region_22.24_spmd.clone.sunk | while | flops 4250867712 | bytes 224271968 | solution.py:117
  830.3 24.4 %bitcast_add_fusion.5 = f32[2048,6,64]{0,2,1:T(8,128)S(1)} fusion(f32[2048,6,64]{0,2,1:T(8,128)S(1)} %copy-done.20, pred[]{:T(512)S(6)} %compare.3, bf16[2048,6,64]{0,2,1:T(8,128)(2,1)S(1)} %copy-done.22, s32[]{:T(128)S(6)} %select_n.138, f32[6,512,2048]{2,1,0:T(8,128)} %fusion.208, f32[6,512]{1,0:T(8,128)S(1)} %constant_dynamic-slice_fusion.2, ...), kind=kOutput, calls=%fused_computation.73.clone.1 | convolution fusion | flops 863502336 | bytes 32915460 | tf_op jit(solution)/shard_map/while/body/eval_jaxpr/hqk,qhe->khe/dot_general | solution.py:110
  865.0 55.9 %fusion.210 = bf16[6,512,2048]{2,1,0:T(8,128)(2,1)} fusion(f32[6,512,2048]{2,1,0:T(8,128)} %fusion.207, f32[6,512,2048]{2,1,0:T(8,128)} %fusion.208, f32[6,512]{1,0:T(8,128)S(1)} %constant_dynamic-slice_fusion.2, pred[512,2048]{1,0:T(8,128)(4,1)S(1)} %fusion.209), kind=kOutput, calls=%fused_computation.65.clone.1 | output fusion | flops 157291520 | bytes 63975424 | tf_op jit(solution)/shard_map/while/body/eval_jaxpr/sub | solution.py:97
  958.2 24.4 %bitcast_add_fusion.5 = f32[2048,6,64]{0,2,1:T(8,128)S(1)} fusion(f32[2048,6,64]{0,2,1:T(8,128)S(1)} %copy-done.20, pred[]{:T(512)S(6)} %compare.3, bf16[2048,6,64]{0,2,1:T(8,128)(2,1)S(1)} %copy-done.22, s32[]{:T(128)S(6)} %select_n.138, f32[6,512,2048]{2,1,0:T(8,128)} %fusion.208, f32[6,512]{1,0:T(8,128)S(1)} %constant_dynamic-slice_fusion.2, ...), kind=kOutput, calls=%fused_computation.73.clone.1 | convolution fusion | flops 863502336 | bytes 32915460 | tf_op jit(solution)/shard_map/while/body/eval_jaxpr/hqk,qhe->khe/dot_general | solution.py:110
  992.9 55.9 %fusion.210 = bf16[6,512,2048]{2,1,0:T(8,128)(2,1)} fusion(f32[6,512,2048]{2,1,0:T(8,128)} %fusion.207, f32[6,512,2048]{2,1,0:T(8,128)} %fusion.208, f32[6,512]{1,0:T(8,128)S(1)} %constant_dynamic-slice_fusion.2, pred[512,2048]{1,0:T(8,128)(4,1)S(1)} %fusion.209), kind=kOutput, calls=%fused_computation.65.clone.1 | output fusion | flops 157291520 | bytes 63975424 | tf_op jit(solution)/shard_map/while/body/eval_jaxpr/sub | solution.py:97
  1087.0 24.4 %bitcast_add_fusion.5 = f32[2048,6,64]{0,2,1:T(8,128)S(1)} fusion(f32[2048,6,64]{0,2,1:T(8,128)S(1)} %copy-done.20, pred[]{:T(512)S(6)} %compare.3, bf16[2048,6,64]{0,2,1:T(8,128)(2,1)S(1)} %copy-done.22, s32[]{:T(128)S(6)} %select_n.138, f32[6,512,2048]{2,1,0:T(8,128)} %fusion.208, f32[6,512]{1,0:T(8,128)S(1)} %constant_dynamic-slice_fusion.2, ...), kind=kOutput, calls=%fused_computation.73.clone.1 | convolution fusion | flops 863502336 | bytes 32915460 | tf_op jit(solution)/shard_map/while/body/eval_jaxpr/hqk,qhe->khe/dot_general | solution.py:110
  1121.7 55.9 %fusion.210 = bf16[6,512,2048]{2,1,0:T(8,128)(2,1)} fusion(f32[6,512,2048]{2,1,0:T(8,128)} %fusion.207, f32[6,512,2048]{2,1,0:T(8,128)} %fusion.208, f32[6,512]{1,0:T(8,128)S(1)} %constant_dynamic-slice_fusion.2, pred[512,2048]{1,0:T(8,128)(4,1)S(1)} %fusion.209), kind=kOutput, calls=%fused_computation.65.clone.1 | output fusion | flops 157291520 | bytes 63975424 | tf_op jit(solution)/shard_map/while/body/eval_jaxpr/sub | solution.py:97
  1215.8 24.4 %bitcast_add_fusion.5 = f32[2048,6,64]{0,2,1:T(8,128)S(1)} fusion(f32[2048,6,64]{0,2,1:T(8,128)S(1)} %copy-done.20, pred[]{:T(512)S(6)} %compare.3, bf16[2048,6,64]{0,2,1:T(8,128)(2,1)S(1)} %copy-done.22, s32[]{:T(128)S(6)} %select_n.138, f32[6,512,2048]{2,1,0:T(8,128)} %fusion.208, f32[6,512]{1,0:T(8,128)S(1)} %constant_dynamic-slice_fusion.2, ...), kind=kOutput, calls=%fused_computation.73.clone.1 | convolution fusion | flops 863502336 | bytes 32915460 | tf_op jit(solution)/shard_map/while/body/eval_jaxpr/hqk,qhe->khe/dot_general | solution.py:110
  1250.4 55.9 %fusion.210 = bf16[6,512,2048]{2,1,0:T(8,128)(2,1)} fusion(f32[6,512,2048]{2,1,0:T(8,128)} %fusion.207, f32[6,512,2048]{2,1,0:T(8,128)} %fusion.208, f32[6,512]{1,0:T(8,128)S(1)} %constant_dynamic-slice_fusion.2, pred[512,2048]{1,0:T(8,128)(4,1)S(1)} %fusion.209), kind=kOutput, calls=%fused_computation.65.clone.1 | output fusion | flops 157291520 | bytes 63975424 | tf_op jit(solution)/shard_map/while/body/eval_jaxpr/sub | solution.py:97
  1447.4 81.5 %all-reduce.1 = (f32[3,384]{1,0:T(4,128)}, f32[1536]{0:T(1024)}) all-reduce(f32[3,384]{1,0:T(4,128)S(1)} %convert_reduce_fusion.1, f32[1536]{0:T(1024)S(1)} %copy-done.43), channel_id=1, replica_groups=mesh['batch'=16,'tensor'=2] {'batch'}, use_global_device_ids=true, to_apply=%region_34.35 | all-reduce | flops 2688 | bytes 21504 | tf_op jit(solution)/shard_map/psum | solution.py:285
  1528.9 41.5 %all-reduce = (f32[768]{0:T(1024)}, f32[768]{0:T(1024)}, f32[768]{0:T(1024)}, f32[768]{0:T(1024)}, f32[768]{0:T(1024)}, /*index=5*/f32[768]{0:T(1024)}) all-reduce(f32[768]{0:T(1024)S(1)} %get-tuple-element.197, f32[768]{0:T(1024)S(1)} %get-tuple-element.202, ...), channel_id=1, replica_groups=mesh['batch'=16,'tensor'=2] {'batch','tensor'}, use_global_device_ids=true, to_apply=%region_29.30 | all-reduce | flops 4608 | bytes 36864 | tf_op jit(solution)/shard_map/psum | solution.py:297
  1575.1 269.5 %all-reduce.5.cloned.1.call-done = (f32[768,3,384]{2,0,1:T(8,128)}, f32[384,768]{1,0:T(8,128)}, f32[768,1536]{1,0:T(8,128)}, f32[1536,768]{1,0:T(8,128)}) async-done(((f32[768,3,384]{2,0,1:T(8,128)}, f32[384,768]{1,0:T(8,128)}, f32[768,1536]{1,0:T(8,128)}, f32[1536,768]{1,0:T(8,128)}), (f32[768,3,384]{2,0,1:T(8,128)}, f32[384,768]{1,0:T(8,128)}, f32[768,1536]{1,0:T(8,128)}, ...) | async-done | bytes 14155792 | tf_op jit(solution)/shard_map/psum | solution.py:285
  (380 shorter events, 782.9 us)
Async XLA Ops:
  7.2 701.8 %copy-start = (bf16[768,1536]{1,0:T(8,128)(2,1)S(1)}, bf16[768,1536]{1,0:T(8,128)(2,1)}, u32[]{:S(2)}) copy-start(bf16[768,1536]{1,0:T(8,128)(2,1)} %param.31) | copy-start | bytes 7077892
  7.2 22.8 %all-gather.6.cloned.1.call-start = ((), (), s32[]{:S(2)}) async-start(), calls=%async_computation.5 | async-start | bytes 4718592 | tf_op jit(solution)/shard_map/all_gather | solution.py:157
  15.0 657.0 %reduce-scatter.6.cloned.1.call-start = ((), (), s32[]{:S(2)}) async-start(), calls=%async_computation.6 | async-start | bytes 9437184 | tf_op jit(solution)/shard_map/reduce_scatter | solution.py:166
  58.2 42.7 %copy-start.2 = (bf16[2048,6,64]{0,2,1:T(8,128)(2,1)S(1)}, bf16[2048,6,64]{0,2,1:T(8,128)(2,1)}, u32[]{:S(2)}) copy-start(bf16[2048,6,64]{0,2,1:T(8,128)(2,1)} %get-tuple-element.531) | copy-start | bytes 4718596 | tf_op jit(solution)/shard_map/while
  140.5 42.7 %copy-start.2 = (bf16[2048,6,64]{0,2,1:T(8,128)(2,1)S(1)}, bf16[2048,6,64]{0,2,1:T(8,128)(2,1)}, u32[]{:S(2)}) copy-start(bf16[2048,6,64]{0,2,1:T(8,128)(2,1)} %get-tuple-element.531) | copy-start | bytes 4718596 | tf_op jit(solution)/shard_map/while
  222.8 42.7 %copy-start.2 = (bf16[2048,6,64]{0,2,1:T(8,128)(2,1)S(1)}, bf16[2048,6,64]{0,2,1:T(8,128)(2,1)}, u32[]{:S(2)}) copy-start(bf16[2048,6,64]{0,2,1:T(8,128)(2,1)} %get-tuple-element.531) | copy-start | bytes 4718596 | tf_op jit(solution)/shard_map/while
  377.4 309.7 %reduce-scatter.10.cloned.1.call-start = ((), (), s32[]{:S(2)}) async-start(), calls=%async_computation.10 | async-start | bytes 9437184 | tf_op jit(solution)/shard_map/reduce_scatter | solution.py:166
  387.0 43.4 %copy-start.3 = (bf16[2048,6,64]{0,2,1:T(8,128)(2,1)S(1)}, bf16[2048,6,64]{0,2,1:T(8,128)(2,1)}, u32[]{:S(2)}) copy-start(bf16[2048,6,64]{0,2,1:T(8,128)(2,1)} %get-tuple-element.501) | copy-start | bytes 4718596 | tf_op jit(solution)/shard_map/while
  457.1 43.1 %copy-start.3 = (bf16[2048,6,64]{0,2,1:T(8,128)(2,1)S(1)}, bf16[2048,6,64]{0,2,1:T(8,128)(2,1)}, u32[]{:S(2)}) copy-start(bf16[2048,6,64]{0,2,1:T(8,128)(2,1)} %get-tuple-element.501) | copy-start | bytes 4718596 | tf_op jit(solution)/shard_map/while
  527.0 43.1 %copy-start.3 = (bf16[2048,6,64]{0,2,1:T(8,128)(2,1)S(1)}, bf16[2048,6,64]{0,2,1:T(8,128)(2,1)}, u32[]{:S(2)}) copy-start(bf16[2048,6,64]{0,2,1:T(8,128)(2,1)} %get-tuple-element.501) | copy-start | bytes 4718596 | tf_op jit(solution)/shard_map/while
  596.9 43.1 %copy-start.3 = (bf16[2048,6,64]{0,2,1:T(8,128)(2,1)S(1)}, bf16[2048,6,64]{0,2,1:T(8,128)(2,1)}, u32[]{:S(2)}) copy-start(bf16[2048,6,64]{0,2,1:T(8,128)(2,1)} %get-tuple-element.501) | copy-start | bytes 4718596 | tf_op jit(solution)/shard_map/while
  671.4 37.6 %all-gather.12.cloned.1.call-start = ((), (), s32[]{:S(2)}) async-start(), calls=%async_computation.11 | async-start | bytes 4718592 | tf_op jit(solution)/shard_map/all_gather | solution.py:175
  672.0 98.9 %copy-start.30 = (f32[768]{0:T(1024)}, f32[768]{0:T(1024)S(1)}, u32[]{:S(2)}) copy-start(f32[768]{0:T(1024)S(1)} %convert_element_type.115) | copy-start | bytes 9220
  695.5 28.2 %all-gather.10.cloned.1.call-start = ((), (), s32[]{:S(2)}) async-start(), calls=%async_computation.9 | async-start | bytes 4718592 | tf_op jit(solution)/shard_map/all_gather | solution.py:217
  696.1 70.4 %reduce-scatter.12.cloned.1.call-start = ((), (), s32[]{:S(2)}) async-start(), calls=%async_computation.12 | async-start | bytes 9437184 | tf_op jit(solution)/shard_map/reduce_scatter | solution.py:230
  750.7 40.3 %all-gather.14.cloned.1.call-start = ((), (), s32[]{:S(2)}) async-start(), calls=%async_computation.13 | async-start | bytes 4718592 | tf_op jit(solution)/shard_map/all_gather | solution.py:241
  777.6 596.1 %reduce-scatter.14.cloned.1.call-start = ((), (), s32[]{:S(2)}) async-start(), calls=%async_computation.14 | async-start | bytes 9437184 | tf_op jit(solution)/shard_map/reduce_scatter | solution.py:268
  1357.9 40.2 %all-gather.8.cloned.1.call-start = ((), (), s32[]{:S(2)}) async-start(), calls=%async_computation.7 | async-start | bytes 4718592 | tf_op jit(solution)/shard_map/all_gather | solution.py:175
  1384.7 185.7 %reduce-scatter.8.cloned.1.call-start = ((), (), s32[]{:S(2)}) async-start(), calls=%async_computation.8 | async-start | bytes 4718592 | tf_op jit(solution)/shard_map/reduce_scatter | solution.py:196
  1412.2 432.4 %all-reduce.5.cloned.1.call-start = ((), (), s32[]{:S(2)}) async-start(), calls=%async_computation.15 | async-start | bytes 28311552 | tf_op jit(solution)/shard_map/psum | solution.py:285
  1444.6 84.3 %copy-start.39 = (f32[768]{0:T(1024)S(1)}, f32[768]{0:T(1024)}, u32[]{:S(2)}) copy-start(f32[768]{0:T(1024)} %get-tuple-element.274) | copy-start | bytes 9220
  1444.6 84.3 %copy-start.40 = (f32[768]{0:T(1024)S(1)}, f32[768]{0:T(1024)}, u32[]{:S(2)}) copy-start(f32[768]{0:T(1024)} %get-tuple-element.286) | copy-start | bytes 9220
  1444.6 84.3 %copy-start.41 = (f32[768]{0:T(1024)S(1)}, f32[768]{0:T(1024)}, u32[]{:S(2)}) copy-start(f32[768]{0:T(1024)} %get-tuple-element.195) | copy-start | bytes 9220
  1444.6 84.3 %copy-start.42 = (f32[768]{0:T(1024)S(1)}, f32[768]{0:T(1024)}, u32[]{:S(2)}) copy-start(f32[768]{0:T(1024)} %get-tuple-element.201) | copy-start | bytes 9220
  (83 other events, 923.1 us)
Sparse Core Ops, SparseCore 0:
  15.2 14.8 all-gather.5
  377.5 15.6 reduce-scatter.5
  671.5 15.6 reduce-scatter.9
  695.7 13.2 all-gather.11
  710.4 13.2 all-gather.9
  750.8 15.6 reduce-scatter.11
  777.7 13.2 all-gather.13
  1358.0 15.6 reduce-scatter.13
  1384.8 13.2 all-gather.7
  1412.4 12.0 reduce-scatter.7
  1444.1 400.4 all-reduce.4
where the time goes:
time: 1870 us; the launch traced here: 1860 us
  matrix products  696 us (37%)
  other arithmetic  549 us (29%)
  waiting for transfers between devices  375 us (20%)
  blocking collectives  123 us (7%)
  local copies, waits for them, and re-layouts  59.6 us (3%)
  loops' own time  43.8 us (2%)
    psum x1, waiting for transfers between devices, on_device(): lax.psum((qkv_weight_grad, qkv_bias_grad, out_weight_grad, fc_weight_grad...  270 us
    sub x4, other arithmetic, one_block(): sign_part * grad_weights - row_dot  224 us
    dot_general x12, matrix products, one_block(): jnp.einsum('qhe,khe->hqk', query_rows, keys, preferred_element_type=jnp.f...  201 us
    dot_general x8, matrix products, one_block(): jnp.einsum('hqk,khe->qhe', weights, values, preferred_element_type=jnp.fl...  172 us
    sub x4, other arithmetic, one_block(): magnitude - largest  171 us
    dot_general x4, matrix products, one_block(): jnp.einsum('hqk,qhe->khe', weights, grad_rows, preferred_element_type=jnp...  97.7 us
    psum x1, blocking collectives, on_device(): lax.psum((qkv_weight_grad, qkv_bias_grad, out_weight_grad, fc_weight_grad...  81.5 us
    reduce_sum x4, other arithmetic, one_block(): total = jnp.sum(exponent, axis=2, keepdims=True)  79.6 us
  transfers between devices with their start and end apart: 11, of which 9 were waited for; matrix products, arithmetic and copies ran while one was open for 18% of the time, Pallas kernels for 0%

commit v1 on v0

v1 whole, which is shorter than its diff:
```python
import functools
import math

import jax
import jax.numpy as jnp
from jax import lax
from jax.experimental import pallas as pl
from jax.experimental.pallas import tpu as pltpu
from jax.sharding import PartitionSpec as P

HEAD_DIM = 64
UNIT = 512
PIECE = 256
UNITS = 16
HALVINGS = 4
CHUNKS = 3
SPLIT = 3
SMALL_ROWS = 72
TALL = 256
STRIP = 16
LOG2E = math.log2(math.e)
MESH = pl.DeviceIdType.MESH
NN = (((1,), (0,)), ((), ()))
NT = (((1,), (1,)), ((), ()))
TN = (((0,), (0,)), ((), ()))


def dot(a, b, dims=NN):
    return lax.dot_general(a, b, dims, preferred_element_type=jnp.float32)


def head_mask(values, head):
    lane = lax.broadcasted_iota(jnp.int32, values.shape, 1)
    keep = (lane >= head * HEAD_DIM) & (lane < (head + 1) * HEAD_DIM)
    return jnp.where(keep, values, jnp.zeros_like(values))


def flipped(me, b):
    return me + (1 - 2 * lax.rem(lax.div(me, 1 << b), 2)) * (1 << b)


def landing_units(bits):
    return UNITS - (UNITS >> min(bits, HALVINGS)) + max(bits - HALVINGS, 0)


def reduction_steps(bits):
    return bits + min(bits, HALVINGS)


def order_of(bits, n):
    rest = list(range(bits - 1))
    turn = n % max(bits - 1, 1)
    return rest[turn:] + rest[:turn] + [bits - 1]


def greet(bits):
    me, core = lax.axis_index("batch"), lax.axis_index("tensor")
    barrier = pltpu.get_barrier_semaphore()
    pl.semaphore_signal(barrier, inc=1, device_id=(me, 1 - core), device_id_type=MESH)
    for b in range(bits):
        pl.semaphore_signal(
            barrier, inc=1, device_id=(flipped(me, b), core), device_id_type=MESH
        )
    pl.semaphore_wait(barrier, bits + 1)


class Reduction:
    def __init__(self, order, parts, sems, base, begin=0, end=None):
        self.order, self.parts, self.base = order, parts, base
        self.send_sems, self.recv_sems, self.keep_sems = sems
        halvings = min(len(order), HALVINGS)
        self.last = UNITS >> halvings
        self.turn = len(order)
        self.steps = [("half", i) for i in range(halvings)]
        self.steps += [("whole", i) for i in range(halvings, len(order))]
        self.steps += [("back", i) for i in reversed(range(halvings))]
        self.begin, self.end = begin, len(self.steps) if end is None else end

    def bit(self, i):
        return lax.rem(lax.div(lax.axis_index("batch"), 1 << self.order[i]), 2)

    def held(self, i):
        start = 0
        for k in range(min(i, HALVINGS)):
            start = start + self.bit(k) * (UNITS >> (k + 1))
        return start

    def slot(self, i):
        offset = 0
        for k in range(i):
            offset += (UNITS >> (k + 1)) if k < HALVINGS else self.last
        return offset

    def copies(self, k):
        kind, i = self.steps[k]
        for index, (data, landing, result) in enumerate(self.parts):
            if kind == "half":
                size = UNITS >> (i + 1)
                source = data(self.held(i) + (1 - self.bit(i)) * size, size)
                target = landing(self.slot(i), size)
            elif kind == "whole":
                source = data(self.held(i), self.last)
                target = landing(self.slot(i), self.last)
            else:
                size = UNITS >> (i + 1)
                source = target = result(self.held(i + 1), size)
                if k == self.turn:
                    source = data(self.held(i + 1), size)
            yield pltpu.make_async_remote_copy(
                src_ref=source,
                dst_ref=target,
                send_sem=self.send_sems.at[self.base + index, k],
                recv_sem=self.recv_sems.at[self.base + index, k],
                device_id=(flipped(lax.axis_index("batch"), self.order[i]), lax.axis_index("tensor")),
                device_id_type=MESH,
            )

    def keeps(self):
        start = self.held(len(self.order))
        for index, (data, _, result) in enumerate(self.parts):
            yield pltpu.make_async_copy(
                data(start, self.last), result(start, self.last), self.keep_sems.at[self.base + index]
            )

    def tick(self, k):
        if k > self.begin:
            kind, i = self.steps[k - 1]
            for copy in self.copies(k - 1):
                copy.wait()
            if k - 1 == self.turn:
                for copy in self.keeps():
                    copy.wait()
            if kind != "back":
                size = UNITS >> (i + 1) if kind == "half" else self.last
                start = self.held(i + 1)
                for data, landing, _ in self.parts:
                    own, came = data(start, size), landing(self.slot(i), size)

                    @pl.loop(0, size)
                    def _(n):
                        own[n] = (
                            own[n].astype(jnp.float32) + came[n].astype(jnp.float32)
                        ).astype(jnp.bfloat16)

        if k >= self.end:
            return
        if k == self.turn:
            for copy in self.keeps():
                copy.start()
        for copy in self.copies(k):
            copy.start()


def views(ref, *lead):
    return lambda start, size: ref.at[(*lead, pl.ds(start, size))]


def chunk_reductions(bits, proj, fc, lead, landed, land, results, base, sems, **limits):
    return [
        Reduction(
            order_of(bits, i),
            [
                (views(proj, lead, i), views(landed[0], land, i), views(results[0], lead, i)),
                (views(fc, lead, i), views(landed[1], land, i), views(results[1], lead, i)),
            ],
            sems,
            base + 2 * i,
            **limits,
        )
        for i in range(SPLIT)
    ]


def strips(rows):
    return [slice(s, s + STRIP) for s in range(0, rows, STRIP)]


def normed(values):
    centred = values - jnp.mean(values, axis=1, keepdims=True)
    rstd = lax.rsqrt(jnp.mean(centred * centred, axis=1, keepdims=True) + 1e-05)
    return centred * rstd, rstd


def norm_back(grad, values, rstd, gain):
    scaled = grad * gain
    inner = (
        scaled
        - jnp.mean(scaled, axis=1, keepdims=True)
        - values * jnp.mean(scaled * values, axis=1, keepdims=True)
    )
    return inner * rstd


def line(ref):
    return ref[...].astype(jnp.float32)[None, :]


def early_kernel(
    x_ref, x_hbm, g_hbm, outw_hbm, w_ref, gain_ref, shift_ref, bias_ref,
    mixed, y1t, x_peer, g_peer, outw_peer,
    x_land, rows_ref, send_sems, recv_sems, store_sem,
):
    wide, half = jnp.float32, jnp.bfloat16
    own = x_ref.shape[0]
    me, core = lax.axis_index("batch"), lax.axis_index("tensor")
    peer = (me, 1 - core)
    barrier = pltpu.get_barrier_semaphore()
    pl.semaphore_signal(barrier, inc=1, device_id=peer, device_id_type=MESH)
    pl.semaphore_wait(barrier, 1)
    swaps = [
        pltpu.make_async_remote_copy(
            src_ref=source, dst_ref=target, send_sem=send_sems.at[n], recv_sem=recv_sems.at[n],
            device_id=peer, device_id_type=MESH,
        )
        for n, (source, target) in enumerate(
            [(x_hbm, x_land), (outw_hbm, outw_peer), (g_hbm, g_peer)]
        )
    ]
    for swap in swaps:
        swap.start()
    gain, shift = line(gain_ref), line(shift_ref)
    local = w_ref.shape[2]

    def rows_of(source, first):
        @pl.loop(0, own // TALL)
        def _(n):
            at = pl.multiple_of(n * TALL, TALL)
            to = pl.ds(pl.multiple_of(first + at, TALL), TALL)
            for cut in strips(TALL):
                values = source[pl.ds(pl.multiple_of(at + cut.start, STRIP), STRIP), :]
                rows_ref[cut, :] = (normed(values.astype(wide))[0] * gain + shift).astype(half)
            for c in range(3):
                cols = slice(c * local, (c + 1) * local)
                result = dot(rows_ref[...], w_ref[c]) + bias_ref[c : c + 1, :].astype(wide)
                if c == 0:
                    result = result * HEAD_DIM**-0.5
                mixed[to, cols] = result.astype(half)
            y1t[:, to] = rows_ref[...].T

    rows_of(x_ref, pl.multiple_of(core * own, own))
    swaps[0].wait()
    store = pltpu.make_async_copy(x_land, x_peer, store_sem.at[0])
    store.start()
    rows_of(x_land, pl.multiple_of((1 - core) * own, own))
    store.wait()
    for swap in swaps[1:]:
        swap.wait()


def early(x, g, outw, w, gain, shift, bias):
    own, width = x.shape
    local = w.shape[2]
    vmem = pl.BlockSpec(memory_space=pltpu.VMEM)
    hbm = pl.BlockSpec(memory_space=pl.ANY)
    dma = pltpu.SemaphoreType.DMA
    shape = jax.ShapeDtypeStruct
    half = jnp.bfloat16
    return pl.pallas_call(
        early_kernel,
        in_specs=[vmem, hbm, hbm, hbm, vmem, vmem, vmem, vmem],
        out_specs=[vmem, vmem, hbm, hbm, hbm],
        out_shape=[
            shape((2 * own, 3 * local), half),
            shape((width, 2 * own), half),
            shape(x.shape, half),
            shape(g.shape, half),
            shape(outw.shape, half),
        ],
        scratch_shapes=[
            pltpu.VMEM(x.shape, half), pltpu.VMEM((TALL, width), half), dma((3,)), dma((3,)), dma((1,)),
        ],
        compiler_params=pltpu.CompilerParams(
            collective_id=2, has_side_effects=True, vmem_limit_bytes=56 * 2**20
        ),
        name="early",
    )(x, x, g, outw, w, gain, shift, bias)


SAFE = 64.0


def attend_forward_kernel(len_ref, q_ref, k_ref, v_ref, ctx_ref, lse_ref, pad_ref, vt_ref, acc_ref, top_ref, sum_ref, score_ref, ratio_ref, weight_ref):
    wide, half = jnp.float32, jnp.bfloat16
    blocks = q_ref.shape[0] // UNIT
    slots = len_ref.shape[1]

    def segment_of(b):
        segment, end = 0, 0
        for j in range(slots):
            end = end + len_ref[0, j]
            segment = segment + jnp.where(b * UNIT >= end, 1, 0)
        return segment

    row = lax.broadcasted_iota(jnp.int32, (128, 128), 0) // HEAD_DIM
    col = lax.broadcasted_iota(jnp.int32, (128, 128), 1) // HEAD_DIM
    same = jnp.where(row == col, 1.0, 0.0).astype(half)
    largest = []
    for ref in (q_ref, k_ref):
        most = jnp.zeros((1, 128), wide)
        for b in range(blocks):
            values = ref[b * UNIT : (b + 1) * UNIT, :]
            norms = dot(values * values, same)
            most = jnp.maximum(most, jnp.max(norms, axis=0, keepdims=True))
        largest.append(most)
    safe = jnp.max(largest[0] * largest[1]) <= SAFE * SAFE
    for b in range(blocks):
        rows = slice(b * UNIT, (b + 1) * UNIT)
        vt_ref[:, rows] = v_ref[rows, :].T

    def one_block(qi, bounded):
        start = pl.multiple_of(qi * UNIT, UNIT)
        query = q_ref[pl.ds(start, UNIT), :]
        turned = query.T
        blank = jnp.zeros((HEAD_DIM, UNIT), half)
        queries = [
            jnp.concatenate([turned[:HEAD_DIM], blank], axis=0),
            jnp.concatenate([blank, turned[HEAD_DIM:]], axis=0),
        ]
        segment = segment_of(qi)
        parts = UNIT // PIECE

        def tile(kj, diagonal):
            spots = []
            for sub in range(parts):
                at = pl.ds(pl.multiple_of(kj * UNIT + sub * PIECE, PIECE), PIECE)
                skip = sub * PIECE if diagonal else 0
                for h in range(2):
                    spots.append((sub * 2 + h, at, skip, h))

            def begin(n, at, skip, h):
                score_ref[n, :, skip:] = dot(k_ref[at, :], queries[h][:, skip:])

            begin(*spots[0])
            for place, (n, at, skip, h) in enumerate(spots):
                if place + 1 < len(spots):
                    begin(*spots[place + 1])
                first = diagonal and skip == 0
                head = slice(h * HEAD_DIM, (h + 1) * HEAD_DIM)
                total = top = jnp.zeros((STRIP, UNIT - skip), wide)

                def kept(size, offset):
                    if not diagonal:
                        return size
                    left = lax.broadcasted_iota(jnp.int32, size.shape, 0) + offset
                    right = lax.broadcasted_iota(jnp.int32, size.shape, 1)
                    keep = (left == right) | ((left < right) & (segment < slots))
                    return jnp.where(keep, size, -1e30)

                totals = {}
                for cut in strips(PIECE):
                    lead = cut.start // 128 * 128 if diagonal and bounded else 0
                    low = skip + lead
                    score = score_ref[n, cut, low:]
                    square = score * score + 1.0
                    inverse = lax.rsqrt(square)
                    size = kept((square * inverse) * LOG2E, cut.start - lead)
                    ratio = score * inverse
                    if bounded:
                        expo = jnp.exp2(size)
                        totals[lead] = totals[lead] + expo if lead in totals else expo
                        weight_ref[n, cut, low:] = (ratio * expo).astype(half)
                        if lead:
                            weight_ref[n, cut, skip:low] = jnp.zeros((STRIP, lead), half)
                    else:
                        top = jnp.maximum(top, size)
                        score_ref[n, cut, skip:] = size
                        ratio_ref[cut, skip:] = ratio
                for lead, part in totals.items():
                    if lead:
                        part = jnp.concatenate([jnp.zeros((STRIP, lead), wide), part], axis=1)
                    total = total + part
                if not bounded:
                    top = jnp.max(top, axis=0, keepdims=True)
                    if not first:
                        old = top_ref[h, :, skip:]
                        top = jnp.maximum(old, top)
                        fade = jnp.exp2(old - top)
                    for cut in strips(PIECE):
                        expo = jnp.exp2(score_ref[n, cut, skip:] - top)
                        total += expo
                        weight_ref[n, cut, skip:] = (ratio_ref[cut, skip:] * expo).astype(half)
                    top_ref[h, :, skip:] = top
                total = jnp.sum(total, axis=0, keepdims=True)
                part = dot(vt_ref[head, at], weight_ref[n, :, skip:])
                if first:
                    sum_ref[h] = total
                    acc_ref[head, :] = part
                elif bounded:
                    sum_ref[h, :, skip:] += total
                    acc_ref[head, skip:] += part
                else:
                    sum_ref[h, :, skip:] = sum_ref[h, :, skip:] * fade + total
                    acc_ref[head, skip:] = acc_ref[head, skip:] * fade + part

        tile(qi, True)

        @pl.loop(0, qi)
        def _(kj):
            @pl.when((segment_of(kj) == segment) & (segment < slots))
            def _():
                tile(kj, False)

        for h in range(2):
            head = slice(h * HEAD_DIM, (h + 1) * HEAD_DIM)
            total = sum_ref[h]
            acc_ref[head, :] = acc_ref[head, :] * (1.0 / total)
            lse = jnp.log2(total)
            if not bounded:
                lse = lse + top_ref[h]
            for kj in range(blocks):
                joined = (qi == kj) | ((segment_of(kj) == segment) & (segment < slots))
                lse_ref[0, h, kj : kj + 1, pl.ds(start, UNIT)] = lse + jnp.where(joined, 0.0, 1e30)
        pad_ref[0:1, pl.ds(start, UNIT)] = jnp.zeros((1, UNIT), wide) + jnp.where(
            segment < slots, 0.0, 1.0
        )
        ctx_ref[pl.ds(start, UNIT), :] = acc_ref[...].T.astype(half)

    @pl.when(safe)
    def _():
        @pl.loop(0, blocks)
        def _(qi):
            one_block(qi, True)

    @pl.when(jnp.logical_not(safe))
    def _():
        @pl.loop(0, blocks)
        def _(qi):
            one_block(qi, False)


def attend_forward(mixed, seq_len):
    count = mixed.shape[0]
    pairs = mixed.shape[1] // (3 * 128)

    def column(group):
        return pl.BlockSpec((count, 128), lambda p, seg: (0, group * pairs + p))

    return pl.pallas_call(
        attend_forward_kernel,
        grid_spec=pltpu.PrefetchScalarGridSpec(
            num_scalar_prefetch=1,
            grid=(pairs,),
            in_specs=[column(0), column(1), column(2)],
            out_specs=[
                pl.BlockSpec((count, 128), lambda p, seg: (0, p)),
                pl.BlockSpec((1, 2, count // UNIT, count), lambda p, seg: (p, 0, 0, 0)),
                pl.BlockSpec((1, count), lambda p, seg: (0, 0)),
            ],
            scratch_shapes=[
                pltpu.VMEM((128, count), jnp.bfloat16),
                pltpu.VMEM((128, UNIT), jnp.float32),
                pltpu.VMEM((2, 1, UNIT), jnp.float32),
                pltpu.VMEM((2, 1, UNIT), jnp.float32),
                pltpu.VMEM((4, PIECE, UNIT), jnp.float32),
                pltpu.VMEM((PIECE, UNIT), jnp.float32),
                pltpu.VMEM((4, PIECE, UNIT), jnp.bfloat16),
            ],
        ),
        out_shape=[
            jax.ShapeDtypeStruct((count, pairs * 128), jnp.bfloat16),
            jax.ShapeDtypeStruct((pairs, 2, count // UNIT, count), jnp.float32),
            jax.ShapeDtypeStruct((1, count), jnp.float32),
        ],
        compiler_params=pltpu.CompilerParams(vmem_limit_bytes=56 * 2**20),
        cost_estimate=pl.CostEstimate(flops=6 * 2 * 2 * 64 * 2048 * 1280, bytes_accessed=8 * 2**20, transcendentals=0),
        name="attend_forward",
    )(seq_len, mixed, mixed, mixed)


def middle_kernel(
    bits, schedule,
    ctx_ref, x_own, x_peer, g_own, g_peer, outw_own, outw_peer, outb_ref, gain_ref, shift_ref, fcw_ref, fcb_ref, projw_ref, projb_ref,
    block_out, gmid_hbm, gctx_ref, outg_ref, projp, fcp, proj_all, fc_all, small_ref,
    x_ref, g_ref, ctx_peer, middle, y2_ref, out_acc, gy_acc, proj_acc, fc_acc, bias_acc, gy_recv, out_recv,
    proj_land, fc_land, proj_zero, fc_zero, fcb_line, pre_ref, grad_ref, hidden_ref, slope_ref, sum_ref,
    load_sems, swap_send, swap_recv, send_sems, recv_sems, keep_sems,
):
    wide, half = jnp.float32, jnp.bfloat16
    count, width = g_ref.shape
    own = count // 2
    blocks = count // UNIT
    heads = ctx_ref.shape[1]
    broad = fcw_ref.shape[1] // CHUNKS
    me, core = lax.axis_index("batch"), lax.axis_index("tensor")
    peer = (me, 1 - core)
    theirs, mine = pl.multiple_of((1 - core) * own, own), pl.multiple_of(core * own, own)
    loads = [
        pltpu.make_async_copy(source, ref.at[pl.ds(start, own)], load_sems.at[n])
        for n, (source, ref, start) in enumerate(
            [(x_own, x_ref, mine), (x_peer, x_ref, theirs), (g_own, g_ref, mine), (g_peer, g_ref, theirs)]
        )
    ]
    for load in loads:
        load.start()
    sems = (send_sems, recv_sems, keep_sems)
    jobs = [
        chunk_reductions(
            bits, proj_zero, fc_zero, 0, (proj_land, fc_land), 0, (proj_all, fc_all), 0, sems
        ),
        chunk_reductions(
            bits, projp, fcp, 0, (proj_land, fc_land), 1, (proj_all, fc_all), 2 * SPLIT, sems,
            end=bits,
        ),
    ]

    def run(spot):
        for n, k in schedule.get(spot, ()):
            for job in jobs[n]:
                job.tick(k)

    def swap(n, source, target):
        return pltpu.make_async_remote_copy(
            src_ref=source, dst_ref=target, send_sem=swap_send.at[n], recv_sem=swap_recv.at[n],
            device_id=peer, device_id_type=MESH,
        )

    greet(bits)
    for b in range(blocks):
        rows = pl.ds(b * UNIT, UNIT)
        swap(b, ctx_ref.at[rows], ctx_peer.at[rows]).start()
    bias_acc[...] = jnp.zeros_like(bias_acc)
    out_acc[...] = jnp.zeros_like(out_acc)
    gy_acc[...] = jnp.zeros_like(gy_acc)
    for load in loads:
        load.wait()
    gain, shift = line(gain_ref), line(shift_ref)
    outb = line(outb_ref)
    fcb_line[...] = line(fcb_ref)

    for b in range(blocks):
        rows = pl.ds(b * UNIT, UNIT)
        swap(b, ctx_ref.at[rows], ctx_peer.at[rows]).wait()

        @pl.loop(0, UNIT // TALL)
        def _(n):
            at = pl.ds(pl.multiple_of(b * UNIT + n * TALL, TALL), TALL)
            middle[at, :] = dot(ctx_ref[at, :], outw_own[...]) + dot(
                ctx_peer[at, :], outw_peer[...]
            )
            for cut in strips(TALL):
                here = pl.ds(pl.multiple_of(b * UNIT + n * TALL + cut.start, STRIP), STRIP)
                values = x_ref[here, :].astype(wide) + middle[here, :] + outb
                middle[here, :] = values
                y2_ref[here, :] = (normed(values)[0] * gain + shift).astype(half)

    root = math.sqrt(2.0 / math.pi)

    @pl.loop(0, CHUNKS * blocks)
    def _(n):
        c, r = lax.div(n, blocks), lax.rem(n, blocks)
        for spot in schedule:
            if isinstance(spot, int):

                @pl.when(n == spot)
                def _(spot=spot):
                    run(spot)

        @pl.when(r == 0)
        def _():
            proj_acc[...] = jnp.zeros_like(proj_acc)
            fc_acc[...] = jnp.zeros_like(fc_acc)

        rows = pl.ds(pl.multiple_of(r * UNIT, UNIT), UNIT)
        cols = pl.ds(pl.multiple_of(c * broad, broad), broad)
        halves = [
            pl.ds(pl.multiple_of(r * UNIT + i * PIECE, PIECE), PIECE) for i in range(UNIT // PIECE)
        ]

        def begin(i):
            pre_ref[i] = dot(y2_ref[halves[i], :], fcw_ref[:, cols])
            grad_ref[i] = dot(g_ref[halves[i], :], projw_ref[cols, :], NT)

        begin(0)
        fcb = fcb_line[:, cols]
        for i, at in enumerate(halves):
            if i + 1 < len(halves):
                begin(i + 1)
            bias = jnp.zeros((STRIP, broad), wide)
            for cut in strips(PIECE):
                pre = pre_ref[i, cut, :] + fcb
                square = pre * pre
                bent = jnp.tanh(pre * (root + (root * 0.044715) * square))
                lift = 0.5 + 0.5 * bent
                hidden_ref[i * PIECE + cut.start : i * PIECE + cut.stop, :] = (pre * lift).astype(half)
                bend = (0.5 * root + (1.5 * root * 0.044715) * square) * (1.0 - bent * bent)
                grad_pre = (grad_ref[i, cut, :] * (lift + pre * bend)).astype(half)
                slope_ref[i * PIECE + cut.start : i * PIECE + cut.stop, :] = grad_pre
                bias += grad_pre.astype(wide)
            bias_acc[c] += jnp.sum(bias, axis=0, keepdims=True)
            cut = slice(i * PIECE, (i + 1) * PIECE)
            out_acc[at, :] += dot(hidden_ref[cut, :], projw_ref[cols, :])
            gy_acc[at, :] += dot(slope_ref[cut, :], fcw_ref[:, cols], NT)
        proj_acc[...] += dot(hidden_ref[...], g_ref[rows, :], TN)
        fc_acc[...] += dot(y2_ref[rows, :], slope_ref[...], TN)

        @pl.when(c == CHUNKS - 1)
        def _():
            x_ref[rows, :] = gy_acc[rows, :].astype(half)
            swap(blocks + r, x_ref.at[rows], gy_recv.at[rows]).start()

        def keep(proj_to, fc_to, slot):
            tall, wing = broad // UNITS, width // SPLIT
            flat = width // UNITS // SPLIT
            for i in range(SPLIT):
                for u in range(UNITS):
                    proj_to[slot, i, u] = proj_acc[
                        u * tall : (u + 1) * tall, i * wing : (i + 1) * wing
                    ].astype(half)
                    row = (u * SPLIT + i) * flat
                    fc_to[slot, i, u] = fc_acc[row : row + flat, :].astype(half)

        @pl.when((r == blocks - 1) & (c == 0))
        def _():
            keep(proj_zero, fc_zero, 0)

        @pl.when((r == blocks - 1) & (c > 0))
        def _():
            keep(projp, fcp, c - 1)

    run("sent")

    @pl.loop(0, own // TALL)
    def _(n):
        at = pl.multiple_of(n * TALL, TALL)
        y2_ref[pl.ds(at, TALL), :] = out_acc[pl.ds(theirs + at, TALL), :].astype(half)

    out_swap = swap(2 * blocks, y2_ref.at[pl.ds(0, own)], out_recv)
    out_swap.start()
    across = width // 128
    fc_acc[:, :heads] = jnp.zeros((width, heads), wide)
    sum_ref[...] = jnp.zeros_like(sum_ref)
    for b in range(count // TALL):
        at = pl.ds(b * TALL, TALL)
        if b % (UNIT // TALL) == 0:
            rows = pl.ds(b * TALL, UNIT)
            swap(blocks + b * TALL // UNIT, x_ref.at[rows], gy_recv.at[rows]).wait()
        run("back%d" % b)
        for cut in strips(TALL):
            here = slice(b * TALL + cut.start, b * TALL + cut.stop)
            grad = x_ref[here, :].astype(wide) + gy_recv[here, :].astype(wide)
            values, rstd = normed(middle[here, :])
            outer = g_ref[here, :].astype(wide)
            total = outer + norm_back(grad, values, rstd, gain)
            gy_acc[here, :] = total
            y2_ref[own + cut.start : own + cut.stop, :] = total.astype(half)
            terms = (total, grad * values, grad, outer)
            for s, term in enumerate(terms):
                sum_ref[s] += term
        gm = y2_ref[own : own + TALL, :]
        gctx_ref[at, :] = dot(gm, outw_own[...], NT).astype(half)
        fc_acc[:, :heads] += dot(gm, ctx_ref[at, :], TN)

    store = pltpu.make_async_copy(gy_acc.at[pl.ds(mine, own)], gmid_hbm, load_sems.at[0])
    store.start()
    outg_ref[...] = fc_acc[:, :heads].astype(half)
    small_ref[...] = jnp.zeros_like(small_ref)
    for i in range(4):
        total = jnp.sum(sum_ref[i], axis=0, keepdims=True)
        for n in range(across):
            small_ref[i * across + n : i * across + n + 1, :] = total[:, n * 128 : (n + 1) * 128]
    for c in range(CHUNKS):
        for n in range(broad // 128):
            row = 4 * across + c * (broad // 128) + n
            small_ref[row : row + 1, :] = bias_acc[c, :, n * 128 : (n + 1) * 128]
    out_swap.wait()
    projb = line(projb_ref)

    @pl.loop(0, own // TALL)
    def _(n):
        at = pl.ds(pl.multiple_of(n * TALL, TALL), TALL)
        from_own = pl.ds(pl.multiple_of(mine + n * TALL, TALL), TALL)
        both = out_acc[from_own, :] + out_recv[at, :].astype(wide)
        block_out[at, :] = (middle[from_own, :] + both + projb).astype(half)

    store.wait()
    run("end")


def middle_plan(bits, blocks):
    plan = {}

    def put(job, total, spots):
        for k in range(total + 1):
            spot = spots[k] if k < min(total, len(spots) - 1) else spots[-1]
            there = plan.setdefault(spot, [])
            there.insert(0 if k == 0 else len(there), (job, k))

    put(0, reduction_steps(bits), [4, 6, 7, 8, 10, 11, "sent", "back2", "end"])
    put(1, bits, [8, 10, "sent", "back3", "end"])
    return plan


def middle(bits, ctx, x, x_peer, g, g_peer, outw, outw_peer, outb, gain, shift, fcw, fcb, projw, projb):
    own, width = g.shape
    count, heads = ctx.shape
    broad = fcw.shape[1] // CHUNKS
    tall, flat, wing = broad // UNITS, width // UNITS // SPLIT, width // SPLIT
    landing, steps = landing_units(bits), reduction_steps(bits)
    half, wide = jnp.bfloat16, jnp.float32
    vmem = pl.BlockSpec(memory_space=pltpu.VMEM)
    hbm = pl.BlockSpec(memory_space=pl.ANY)
    dma = pltpu.SemaphoreType.DMA
    shape = jax.ShapeDtypeStruct
    return pl.pallas_call(
        functools.partial(middle_kernel, bits, middle_plan(bits, count // UNIT)),
        in_specs=[vmem] + [hbm] * 4 + [vmem] * 9,
        out_specs=[vmem, hbm, vmem, vmem, vmem, vmem, hbm, hbm, vmem],
        out_shape=[
            shape((own, width), half),
            shape((own, width), wide),
            shape((count, heads), half),
            shape((width, heads), half),
            shape((CHUNKS - 1, SPLIT, UNITS, tall, wing), half),
            shape((CHUNKS - 1, SPLIT, UNITS, flat, broad), half),
            shape((1, SPLIT, UNITS, tall, wing), half),
            shape((1, SPLIT, UNITS, flat, broad), half),
            shape((40, 128), wide),
        ],
        scratch_shapes=[
            pltpu.VMEM((count, width), half),
            pltpu.VMEM((count, width), half),
            pltpu.VMEM((count, heads), half),
            pltpu.VMEM((count, width), wide),
            pltpu.VMEM((count, width), half),
            pltpu.VMEM((count, width), wide),
            pltpu.VMEM((count, width), wide),
            pltpu.VMEM((broad, width), wide),
            pltpu.VMEM((width, broad), wide),
            pltpu.VMEM((CHUNKS, 1, broad), wide),
            pltpu.VMEM((count, width), half),
            pltpu.VMEM((own, width), half),
            pltpu.VMEM((2, SPLIT, landing, tall, wing), half),
            pltpu.VMEM((2, SPLIT, landing, flat, broad), half),
            pltpu.VMEM((1, SPLIT, UNITS, tall, wing), half),
            pltpu.VMEM((1, SPLIT, UNITS, flat, broad), half),
            pltpu.VMEM((1, CHUNKS * broad), wide),
            pltpu.VMEM((UNIT // PIECE, PIECE, broad), wide),
            pltpu.VMEM((UNIT // PIECE, PIECE, broad), wide),
            pltpu.VMEM((UNIT, broad), half),
            pltpu.VMEM((UNIT, broad), half),
            pltpu.VMEM((4, STRIP, width), wide),
            dma((4,)),
            dma((2 * (count // UNIT) + 1,)),
            dma((2 * (count // UNIT) + 1,)),
            dma((4 * SPLIT, steps)),
            dma((4 * SPLIT, steps)),
            dma((4 * SPLIT,)),
        ],
        compiler_params=pltpu.CompilerParams(
            collective_id=1, has_side_effects=True, vmem_limit_bytes=63 * 2**20
        ),
        name="middle",
    )(ctx, x, x_peer, g, g_peer, outw, outw_peer, outb, gain, shift, fcw, fcb, projw, projb)


def late_kernel(
    bits, schedule,
    q_ref, go_ref, ctx_ref, lse_ref, pad_ref, y1t_hbm, qkvw_hbm, projp_hbm, fcp_hbm, outg_ref,
    x_hbm, gmid_hbm, gain_ref, small_ref,
    proj_all, fc_all, pair_all, igrad, small,
    y1t, qkvw, x_ref, gmid, gmix, kt_ref, dqt_ref, dk_acc, dv_acc, dot_ref, part_own,
    part_send, part_recv, proj_part, fc_part, pair_part, proj_land, fc_land, pair_land, small_recv, pair_out,
    qt_ref, gt_ref, qm_ref, gm_ref, score_ref, dw_ref, weight_ref, slope_ref, sum_ref,
    load_sems, keep_sems, send_sems, recv_sems, pair_sems, small_send, small_got,
):
    wide, half = jnp.float32, jnp.bfloat16
    count = q_ref.shape[0]
    blocks = count // UNIT
    pairs = ctx_ref.shape[1] // 128
    sets = proj_part.shape[0]
    own = x_hbm.shape[0]
    me, core = lax.axis_index("batch"), lax.axis_index("tensor")
    peer = (me, 1 - core)

    loads = [
        pltpu.make_async_copy(source, target, load_sems.at[n])
        for n, (source, target) in enumerate(
            [
                (projp_hbm, proj_part),
                (fcp_hbm, fc_part),
                (y1t_hbm, y1t), (qkvw_hbm, qkvw), (x_hbm, x_ref), (gmid_hbm, gmid),
            ]
        )
    ]
    for load in loads:
        load.start()

    sems = (send_sems, recv_sems, keep_sems)
    jobs = []
    for c in range(sets):
        jobs.append(
            chunk_reductions(
                bits, proj_part, fc_part, c, (proj_land, fc_land), c, (proj_all, fc_all),
                2 * SPLIT * c, sems, begin=bits if c == 0 else 0,
            )
        )
    for p in range(pairs):
        jobs.append(
            [
                Reduction(
                    order_of(bits, i),
                    [tuple(views(ref, p, i) for ref in (pair_part, pair_land, pair_all))],
                    sems,
                    2 * SPLIT * sets + SPLIT * p + i,
                )
                for i in range(SPLIT)
            ]
        )

    def run(spot):
        for n, k in schedule.get(spot, ()):
            for job in jobs[n]:
                job.tick(k)

    greet(bits)
    loads[0].wait()
    loads[1].wait()
    run("start")
    loads[2].wait()

    small[0:32, :] = jnp.zeros((32, 128), wide)
    small[32:SMALL_ROWS, :] = small_ref[...]

    def columns(group, p):
        return pl.ds(pl.multiple_of((group * pairs + p) * 128, 128), 128)

    turns = blocks * (blocks + 1) // 2
    flat = pair_part.shape[3]

    def spread(p, source, cols, to):
        for u in range(UNITS):
            for i in range(SPLIT):
                row = (u * SPLIT + i) * flat
                pair_part[p, i, u, :, to] = source[row : row + flat, cols]

    @pl.loop(0, pairs * turns)
    def _(n):
        p, m = lax.div(n, turns), lax.rem(n, turns)
        qi = 0
        for b in range(1, blocks):
            qi = qi + jnp.where(m >= b * (b + 1) // 2, 1, 0)
        j = m - lax.div(qi * (qi + 1), 2)
        for spot in schedule:
            if isinstance(spot, int):

                @pl.when(n == spot)
                def _(spot=spot):
                    run(spot)

        lanes = columns(0, p)

        @pl.when(m == 0)
        def _():
            for b in range(blocks):
                rows = slice(b * UNIT, (b + 1) * UNIT)
                kt_ref[:, rows] = q_ref[rows, columns(1, p)].T
                product = (go_ref[rows, lanes].astype(wide) * ctx_ref[rows, lanes].astype(wide)).T
                for h in range(2):
                    head = slice(h * HEAD_DIM, (h + 1) * HEAD_DIM)
                    dot_ref[h, :, rows] = jnp.sum(product[head, :], axis=0, keepdims=True)

        start = pl.multiple_of(qi * UNIT, UNIT)
        here = pl.ds(start, UNIT)

        @pl.when(j == 0)
        def _():
            blank = jnp.zeros((HEAD_DIM, UNIT), half)
            for ref, turned, masked in ((q_ref, qt_ref, qm_ref), (go_ref, gt_ref, gm_ref)):
                values = ref[here, lanes]
                turn = values.T
                for h in range(2):
                    head = slice(h * HEAD_DIM, (h + 1) * HEAD_DIM)
                    rest = slice((1 - h) * HEAD_DIM, (2 - h) * HEAD_DIM)
                    turned[h, head, :] = turn[head]
                    turned[h, rest, :] = blank
                    masked[h] = head_mask(values, h)

        def tile(kj, diagonal):
            spots = []
            for sub in range(UNIT // PIECE):
                at = pl.ds(pl.multiple_of(kj * UNIT + sub * PIECE, PIECE), PIECE)
                skip = sub * PIECE if diagonal else 0
                for h in range(2):
                    spots.append((sub * 2 + h, at, skip, h))

            def begin(n, at, skip, h):
                score_ref[n, :, skip:] = dot(q_ref[at, columns(1, p)], qt_ref[h, :, skip:])
                dw_ref[n, :, skip:] = dot(q_ref[at, columns(2, p)], gt_ref[h, :, skip:])

            begin(*spots[0])
            for place, (n, at, skip, h) in enumerate(spots):
                if place + 1 < len(spots):
                    begin(*spots[place + 1])
                head = slice(h * HEAD_DIM, (h + 1) * HEAD_DIM)
                span = pl.ds(pl.multiple_of(start + skip, PIECE), UNIT - skip)
                lse = lse_ref[p, h, pl.ds(kj, 1), span]
                rowdot = dot_ref[h, :, span]
                if diagonal:
                    free = pad_ref[0:1, span] < 0.5
                for cut in strips(PIECE):
                    lead = cut.start // 128 * 128 if diagonal else 0
                    low = skip + lead
                    score = score_ref[n, cut, low:]
                    square = score * score + 1.0
                    inverse = lax.rsqrt(square)
                    size = (square * inverse) * LOG2E - lse[:, lead:]
                    if diagonal:
                        left = lax.broadcasted_iota(jnp.int32, size.shape, 0) + (cut.start - lead)
                        right = lax.broadcasted_iota(jnp.int32, size.shape, 1)
                        keep = (left == right) | ((left < right) & free[:, lead:])
                        size = jnp.where(keep, size, -1e30)
                    ratio = score * inverse
                    prob = jnp.exp2(size)
                    weight_ref[n, cut, low:] = (ratio * prob).astype(half)
                    factor = 1.0 + (inverse * inverse) * (inverse - 1.0)
                    slope_ref[n, cut, low:] = (
                        prob * (dw_ref[n, cut, low:] * factor - ratio * rowdot[:, lead:])
                    ).astype(half)
                    if lead:
                        blank = jnp.zeros((STRIP, lead), half)
                        weight_ref[n, cut, skip:low] = blank
                        slope_ref[n, cut, skip:low] = blank
                dv_new = dot(weight_ref[n, :, skip:], gm_ref[h, skip:, :])
                dk_new = dot(slope_ref[n, :, skip:], qm_ref[h, skip:, :])
                dq_new = dot(kt_ref[head, at], slope_ref[n, :, skip:])
                if diagonal and skip == 0:
                    dqt_ref[head, :] = dq_new
                else:
                    dqt_ref[head, skip:] += dq_new
                if diagonal and h == 0:
                    dk_acc[at, :] = dk_new
                    dv_acc[at, :] = dv_new
                else:
                    dk_acc[at, :] += dk_new
                    dv_acc[at, :] += dv_new

        @pl.when(j == 0)
        def _():
            tile(qi, True)

        @pl.when(j > 0)
        def _():
            tile(j - 1, False)

        @pl.when(j == qi)
        def _():
            gmix[here, lanes] = (dqt_ref[...].T * HEAD_DIM**-0.5).astype(half)

        @pl.when(m == turns - 1)
        def _():
            gmix[:, columns(1, p)] = dk_acc[...].astype(half)
            gmix[:, columns(2, p)] = dv_acc[...].astype(half)
            for g in range(3):
                block = gmix[:, columns(g, p)]
                total = jnp.zeros((STRIP, 128), wide)
                for cut in strips(count):
                    total += gmix[cut, columns(g, p)].astype(wide)
                small[pl.ds(16 + g * pairs + p, 1), :] = jnp.sum(total, axis=0, keepdims=True)
                pair_out[...] = dot(y1t[...], block).astype(half)
                spread(p, pair_out, slice(None), slice(g * 128, (g + 1) * 128))
            spread(p, outg_ref, lanes, slice(384, 512))

    run("after")
    for load in loads[3:]:
        load.wait()
    tall = 256
    theirs, mine = (1 - core) * own, core * own
    local = qkvw.shape[2]

    def back(first):
        rows = pl.ds(pl.multiple_of(first, tall), tall)
        return sum(
            dot(gmix[rows, g * local : (g + 1) * local], qkvw[g], NT) for g in range(3)
        )

    @pl.loop(0, own // tall)
    def _(r):
        at = pl.multiple_of(r * tall, tall)
        part_send[pl.ds(at, tall), :] = back(theirs + at).astype(half)

    swap = pltpu.make_async_remote_copy(
        src_ref=part_send, dst_ref=part_recv, send_sem=pair_sems.at[0], recv_sem=pair_sems.at[1],
        device_id=peer, device_id_type=MESH,
    )
    swap.start()
    run("sent")

    @pl.loop(0, own // tall)
    def _(r):
        at = pl.multiple_of(r * tall, tall)
        part_own[pl.ds(at, tall), :] = back(mine + at)

    run("own")
    swap.wait()
    gain = line(gain_ref)
    sum_ref[...] = jnp.zeros_like(sum_ref)

    for r in range(own // TALL):
        run("norm%d" % r)
        for cut in strips(TALL):
            rows = slice(r * TALL + cut.start, r * TALL + cut.stop)
            values, rstd = normed(x_ref[rows, :].astype(wide))
            grad = part_own[rows, :] + part_recv[rows, :].astype(wide)
            igrad[rows, :] = (gmid[rows, :] + norm_back(grad, values, rstd, gain)).astype(half)
            sum_ref[0] += grad * values
            sum_ref[1] += grad

    gain_sum = jnp.sum(sum_ref[0], axis=0, keepdims=True)
    bias_sum = jnp.sum(sum_ref[1], axis=0, keepdims=True)
    across = x_ref.shape[1] // 128
    for n in range(across):
        small[n : n + 1, :] = gain_sum[:, n * 128 : (n + 1) * 128]
        small[across + n : across + n + 1, :] = bias_sum[:, n * 128 : (n + 1) * 128]
    run("normed")

    for k in range(bits + 1):
        partner = peer if k == 0 else (flipped(me, k - 1), core)
        copy = pltpu.make_async_remote_copy(
            src_ref=small, dst_ref=small_recv.at[k], send_sem=small_send.at[k],
            recv_sem=small_got.at[k], device_id=partner, device_id_type=MESH,
        )
        copy.start()
        run("small%d" % k)
        copy.wait()
        if k == 0:
            small[0:16, :] += small_recv[0, 0:16, :]
        else:
            small[...] += small_recv[k]
    run("end")


def late_plan(bits, sets, pairs, turns):
    plan = {}

    def put(job, spots, begin=0):
        total = reduction_steps(bits) - begin
        for k in range(total + 1):
            spot = spots[k] if k < min(total, len(spots) - 1) else spots[-1]
            there = plan.setdefault(spot, [])
            there.insert(0 if k == 0 else len(there), (job, begin + k))

    put(0, ["start", 3, 5, 8, 12], bits)
    put(1, ["start", 5, 8, 10, 13, 16, 18, 21, 25])
    put(2, [turns, 14, 16, 18, 20, 22, 24, 26, 29])
    put(3, [2 * turns, 23, 25, 27, 29, "after", "own", "norm1", "normed"])
    put(4, ["after", "own", "norm1", "norm3", "small0", "small1", "small2", "small3", "end"])
    return plan


def late(bits, mixed, grad_context, context, lse, padded, y1t, qkvw, projp, fcp, outg, x, gmid, gain, small):
    count, width = mixed.shape[0], y1t.shape[0]
    pairs = context.shape[1] // 128
    own = x.shape[0]
    sets = CHUNKS - 1
    tall, wing = projp.shape[3:]
    flat, broad = fcp.shape[3:]
    landing, steps = landing_units(bits), reduction_steps(bits)
    blocks = count // UNIT
    parts = SPLIT * (2 * sets + pairs)
    half, wide = jnp.bfloat16, jnp.float32
    vmem = pl.BlockSpec(memory_space=pltpu.VMEM)
    hbm = pl.BlockSpec(memory_space=pl.ANY)
    dma = pltpu.SemaphoreType.DMA
    return pl.pallas_call(
        functools.partial(
            late_kernel, bits, late_plan(bits, sets, pairs, blocks * (blocks + 1) // 2)
        ),
        in_specs=[vmem, vmem, vmem, vmem, vmem, hbm, hbm, hbm, hbm, vmem, hbm, hbm, vmem, vmem],
        out_specs=[hbm, hbm, hbm, vmem, vmem],
        out_shape=[
            jax.ShapeDtypeStruct((sets, SPLIT, UNITS, tall, wing), half),
            jax.ShapeDtypeStruct((sets, SPLIT, UNITS, flat, broad), half),
            jax.ShapeDtypeStruct((pairs, SPLIT, UNITS, flat, 512), half),
            jax.ShapeDtypeStruct((own, width), half),
            jax.ShapeDtypeStruct((SMALL_ROWS, 128), wide),
        ],
        scratch_shapes=[
            pltpu.VMEM(y1t.shape, half),
            pltpu.VMEM(qkvw.shape, half),
            pltpu.VMEM(x.shape, half),
            pltpu.VMEM(gmid.shape, wide),
            pltpu.VMEM(mixed.shape, half),
            pltpu.VMEM((128, count), half),
            pltpu.VMEM((128, UNIT), wide),
            pltpu.VMEM((count, 128), wide),
            pltpu.VMEM((count, 128), wide),
            pltpu.VMEM((2, 1, count), wide),
            pltpu.VMEM((own, width), wide),
            pltpu.VMEM((own, width), half),
            pltpu.VMEM((own, width), half),
            pltpu.VMEM((sets, SPLIT, UNITS, tall, wing), half),
            pltpu.VMEM((sets, SPLIT, UNITS, flat, broad), half),
            pltpu.VMEM((pairs, SPLIT, UNITS, flat, 512), half),
            pltpu.VMEM((sets, SPLIT, landing, tall, wing), half),
            pltpu.VMEM((sets, SPLIT, landing, flat, broad), half),
            pltpu.VMEM((pairs, SPLIT, landing, flat, 512), half),
            pltpu.VMEM((bits + 1, SMALL_ROWS, 128), wide),
            pltpu.VMEM((width, 128), half),
            pltpu.VMEM((2, 128, UNIT), half),
            pltpu.VMEM((2, 128, UNIT), half),
            pltpu.VMEM((2, UNIT, 128), half),
            pltpu.VMEM((2, UNIT, 128), half),
            pltpu.VMEM((4, PIECE, UNIT), wide),
            pltpu.VMEM((4, PIECE, UNIT), wide),
            pltpu.VMEM((4, PIECE, UNIT), half),
            pltpu.VMEM((4, PIECE, UNIT), half),
            pltpu.VMEM((2, STRIP, width), wide),
            dma((6,)),
            dma((parts,)),
            dma((parts, steps)),
            dma((parts, steps)),
            dma((2,)),
            dma((bits + 1,)),
            dma((bits + 1,)),
        ],
        compiler_params=pltpu.CompilerParams(
            collective_id=0, has_side_effects=True, vmem_limit_bytes=62 * 2**20
        ),
        name="late",
    )(
        mixed, grad_context, context, lse, padded, y1t, qkvw, projp, fcp, outg, x, gmid, gain, small
    )


def finish_kernel(proj_first, proj_rest, fc_first, fc_rest, pair_ref, out_ref, small, rows_in, grads_in, rows_out, grads_out, proj, fc, qkv, outw, *lines):
    wide = jnp.float32
    pairs = pair_ref.shape[0]
    rows_out[...] = rows_in[...]
    grads_out[...] = grads_in[...]
    step, flat, broad = fc_rest.shape[2:]
    wing = proj_rest.shape[4]
    ahead = fc_first.shape[0]
    for c in range(CHUNKS):
        first = c < ahead
        proj_from, fc_from = (proj_first, fc_first) if first else (proj_rest, fc_rest)
        at = c if first else c - ahead
        for i in range(SPLIT):
            for s in range(step):
                proj[c, s, :, i * wing : (i + 1) * wing] = proj_from[at, i, s].astype(wide)
                row = (s * SPLIT + i) * flat
                fc[row : row + flat, c * broad : (c + 1) * broad] = fc_from[at, i, s].astype(wide)
    for i in range(SPLIT):
        for s in range(step):
            row = (s * SPLIT + i) * flat
            for p in range(pairs):
                for c in range(3):
                    qkv[c, row : row + flat, p * 128 : (p + 1) * 128] = pair_ref[
                        p, i, s, :, c * 128 : (c + 1) * 128
                    ].astype(wide)

    @pl.when(pl.program_id(0) == 0)
    def _():
        for p in range(pairs):
            for block in range(UNITS * SPLIT * flat // 128):
                rows = []
                for row in range(block * 128, (block + 1) * 128, flat):
                    u, i = divmod(row // flat, SPLIT)
                    rows.append(out_ref[p, i, u].astype(wide))
                outw[p * 128 : (p + 1) * 128, block * 128 : (block + 1) * 128] = jnp.concatenate(
                    rows, axis=0
                ).T
        across = proj.shape[3] // 128
        for g in range(3):
            for p in range(pairs):
                row = 16 + g * pairs + p
                lines[0][g : g + 1, p * 128 : (p + 1) * 128] = small[row : row + 1, :]
        first = 0
        for i, target in enumerate(lines[1:]):
            if i == 2:
                first = 32
            for n in range(target.shape[0] // 128):
                target[pl.ds(n * 128, 128)] = small[first + n]
            first += target.shape[0] // 128


def finish(proj_first, proj_rest, fc_first, fc_rest, pair_all, small, block_out, input_grad):
    ahead, _, _, tall, wing = proj_first.shape
    flat, broad = fc_first.shape[3:]
    width = wing * SPLIT
    high = flat * SPLIT
    pairs = pair_all.shape[0]
    step = 2
    wide = jnp.float32
    shape = jax.ShapeDtypeStruct
    rows = pl.BlockSpec((block_out.shape[0] * step // UNITS, width), lambda u: (u, 0))
    lengths = [width] * 6 + [CHUNKS * broad]
    block_out, input_grad, proj, fc, qkv, outw, *lines = pl.pallas_call(
        finish_kernel,
        grid=(UNITS // step,),
        in_specs=[
            pl.BlockSpec((ahead, SPLIT, step, tall, wing), lambda u: (0, 0, u, 0, 0)),
            pl.BlockSpec((CHUNKS - ahead, SPLIT, step, tall, wing), lambda u: (0, 0, u, 0, 0)),
            pl.BlockSpec((ahead, SPLIT, step, flat, broad), lambda u: (0, 0, u, 0, 0)),
            pl.BlockSpec((CHUNKS - ahead, SPLIT, step, flat, broad), lambda u: (0, 0, u, 0, 0)),
            pl.BlockSpec((pairs, SPLIT, step, flat, 384), lambda u: (0, 0, u, 0, 0)),
            pl.BlockSpec((pairs, SPLIT, UNITS, flat, 128), lambda u: (0, 0, 0, 0, 3)),
            pl.BlockSpec((SMALL_ROWS, 128), lambda u: (0, 0)),
            rows,
            rows,
        ],
        out_specs=[
            rows,
            rows,
            pl.BlockSpec((CHUNKS, step, tall, width), lambda u: (0, u, 0, 0)),
            pl.BlockSpec((step * high, CHUNKS * broad), lambda u: (u, 0)),
            pl.BlockSpec((3, step * high, pairs * 128), lambda u: (0, u, 0)),
            pl.BlockSpec((pairs * 128, width), lambda u: (0, 0)),
            pl.BlockSpec((3, pairs * 128), lambda u: (0, 0)),
        ]
        + [pl.BlockSpec((length,), lambda u: (0,)) for length in lengths],
        out_shape=[
            shape(block_out.shape, block_out.dtype),
            shape(input_grad.shape, input_grad.dtype),
            shape((CHUNKS, UNITS, tall, width), wide),
            shape((width, CHUNKS * broad), wide),
            shape((3, width, pairs * 128), wide),
            shape((pairs * 128, width), wide),
            shape((3, pairs * 128), wide),
        ]
        + [shape((length,), wide) for length in lengths],
        compiler_params=pltpu.CompilerParams(vmem_limit_bytes=61 * 2**20),
        name="finish",
    )(proj_first, proj_rest, fc_first, fc_rest, pair_all, pair_all, small, block_out, input_grad)
    return block_out, input_grad, proj.reshape(-1, width), fc, jnp.transpose(qkv, (1, 0, 2)), outw, lines


def on_device(
    block_in, seq_len, ln1_gain, ln1_bias, qkv_weight, qkv_bias, out_weight, out_bias,
    ln2_gain, ln2_bias, fc_weight, fc_bias, proj_weight, proj_bias, cotangent,
):
    bits = lax.axis_size("batch").bit_length() - 1
    qkv = jnp.transpose(qkv_weight, (1, 0, 2))
    mixed, y1t, x_peer, g_peer, outw_peer = early(
        block_in, cotangent, out_weight, qkv, ln1_gain, ln1_bias, qkv_bias
    )
    context, lse, padded = attend_forward(mixed, seq_len)
    (
        block_out, grad_middle, grad_context, out_grad, proj_parts, fc_parts, proj_first, fc_first, small,
    ) = middle(
        bits, context, block_in, x_peer, cotangent, g_peer, out_weight, outw_peer,
        out_bias, ln2_gain, ln2_bias, fc_weight, fc_bias, proj_weight, proj_bias,
    )
    proj_rest, fc_rest, pair_all, input_grad, small = late(
        bits, mixed, grad_context, context, lse, padded, y1t, qkv,
        proj_parts, fc_parts, out_grad, block_in, grad_middle, ln1_gain, small,
    )
    block_out, input_grad, proj_grad, fc_grad, qkv_grad, outw_grad, lines = finish(
        proj_first, proj_rest, fc_first, fc_rest, pair_all, small, block_out, input_grad
    )
    (
        qkv_bias_grad, gain_one_grad, shift_one_grad, out_bias_grad, gain_two_grad, shift_two_grad,
        proj_bias_grad, fc_bias_grad,
    ) = lines
    return (
        block_out,
        input_grad,
        gain_one_grad,
        shift_one_grad,
        qkv_grad,
        qkv_bias_grad,
        outw_grad,
        out_bias_grad,
        gain_two_grad,
        shift_two_grad,
        fc_grad,
        fc_bias_grad,
        proj_grad,
        proj_bias_grad,
    )


def solution(mesh):
    placed = (
        P(("batch", "tensor"), None),
        P("batch", None),
        P(),
        P(),
        P(None, None, "tensor"),
        P(None, "tensor"),
        P("tensor", None),
        P(),
        P(),
        P(),
        P(None, "tensor"),
        P("tensor"),
        P("tensor", None),
        P(),
        P(("batch", "tensor"), None),
    )
    return jax.shard_map(
        on_device,
        mesh=mesh,
        in_specs=placed,
        out_specs=(
            P(("batch", "tensor"), None),
            P(("batch", "tensor"), None),
            P(),
            P(),
            P(None, None, "tensor"),
            P(None, "tensor"),
            P("tensor", None),
            P(),
            P(),
            P(),
            P(None, "tensor"),
            P("tensor"),
            P("tensor", None),
            P(),
        ),
        check_vma=False,
    )
```

time: 1870 us -> 280 us (0.15)
  matrix products: 696 us -> 0 us
  other arithmetic: 549 us -> 0 us
  waiting for transfers between devices: 375 us -> 0 us
  Pallas kernels: 0 us -> 278 us
  blocking collectives: 123 us -> 0 us
  local copies, waits for them, and re-layouts: 59.6 us -> 0 us
  loops' own time: 43.8 us -> 0 us
    dot_general x49 -> x0, matrix products: 696 us -> none  [the longest x12 201 us: one_block(): jnp.einsum('qhe,khe->hqk', query_rows, keys, preferred_element_type=jnp.f...]
    sub x8 -> x0, other arithmetic: 395 us -> none  [the longest x4 224 us: one_block(): sign_part * grad_weights - row_dot]
    pallas_call x0 -> x5, Pallas kernels: none -> 278 us  [the longest x1 133 us: late(): pl.pallas_call(functools.partial(late_kernel, bits, late_plan(bits, sets,...]
    psum x1 -> x0, waiting for transfers between devices: 270 us -> none  [on_device(): lax.psum((qkv_weight_grad, qkv_bias_grad, out_weight_grad, fc_weight_grad...]
    psum x2 -> x0, blocking collectives: 123 us -> none  [the longest x1 81.5 us: on_device(): lax.psum((qkv_weight_grad, qkv_bias_grad, out_weight_grad, fc_weight_grad...]
    reduce_sum x13 -> x0, other arithmetic: 104 us -> none  [the longest x4 79.6 us: one_block(): total = jnp.sum(exponent, axis=2, keepdims=True)]
    all_gather x5 -> x0, waiting for transfers between devices: 58.8 us -> none  [the longest x2 26.2 us: attention_half(): lax.all_gather(norm_two.astype(half_type), 'tensor', axis=0, tiled=True)]
    reduce_scatter x5 -> x0, waiting for transfers between devices: 46 us -> none  [the longest x1 15.8 us: on_device(): lax.psum_scatter(jnp.einsum('cf,df->cd', grad_pre, fc_weight, preferred_e...]
  transfers between devices with their start and end apart: 11 -> 0, of which waited for: 9 -> 0; matrix products, arithmetic and copies ran while one was open for 18% -> 0% of each run, Pallas kernels for 0% -> 0%
where the time goes in v1:
time: 280 us; the launch traced here: 279 us
  Pallas kernels  278 us (99%)
    pallas_call x1, Pallas kernels, late(): pl.pallas_call(functools.partial(late_kernel, bits, late_plan(bits, sets,...  133 us
    pallas_call x1, Pallas kernels, middle(): pl.pallas_call(functools.partial(middle_kernel, bits, middle_plan(bits, c...  96.6 us
    pallas_call x1, Pallas kernels, attend_forward(): pl.pallas_call(attend_forward_kernel, grid_spec=pltpu.PrefetchScalarGridS...  20.6 us
    pallas_call x1, Pallas kernels, early(): pl.pallas_call(early_kernel, in_specs=[vmem, hbm, hbm, hbm, vmem, vmem, v...  15.2 us
    pallas_call x1, Pallas kernels, finish(): pl.pallas_call(finish_kernel, grid=(UNITS // step,), in_specs=[pl.BlockSp...  12.1 us

profile of v1, /device:TPU:0, one launch (start us, length us, event | category | flops | bytes accessed | tf_op | source)
XLA Modules:
  0.0 278.7 jit_solution(8768861355079133626)
XLA Ops:
  0.6 15.2 %early.1 = (bf16[2048,1152]{1,0:T(8,128)(2,1)}, bf16[768,2048]{1,0:T(8,128)(2,1)}, bf16[1024,768]{1,0:T(8,128)(2,1)}, bf16[1024,768]{1,0:T(8,128)(2,1)}, bf16[384,768]{1,0:T(8,128)(2,1)}) custom-call(bf16[1024,768]{1,0:T(8,128)(2,1)} %x_hbm.3, bf16[1024,768]{1,0:T(8,128)(2,1)} %x_hbm.3, bf16[1024,768]{1,0:T(8,128)(2,1)} %g_own.1, bf16[384,768]{1,0:T(8,128)(2,1)} %outw_own.1, ...), custom_call_target="tpu_custom_call" | custom-call | tf_op jit(solution)/shard_map/early/pallas_call | solution.py:258
  15.9 20.6 %attend_forward.1 = (bf16[2048,384]{1,0:T(8,128)(2,1)}, f32[3,2,4,2048]{3,2,1,0:T(4,128)}, f32[1,2048]{1,0:T(1,128)}) custom-call(s32[1,4]{1,0:T(1,128)} %len_ref.1, bf16[2048,1152]{1,0:T(8,128)(2,1)} %get-tuple-element.50.q_ref.k_ref.v_ref, bf16[2048,1152]{1,0:T(8,128)(2,1)} %get-tuple-element.50.q_ref.k_ref.v_ref, ...), custom_call_target="tpu_custom_call" | custom-call | flops 4026531840 | bytes 8388608 | tf_op jit(solution)/shard_map/attend_forward/pallas_call | solution.py:438
  36.5 96.6 %middle.1 = (bf16[1024,768]{1,0:T(8,128)(2,1)}, f32[1024,768]{1,0:T(8,128)}, bf16[2048,384]{1,0:T(8,128)(2,1)}, bf16[768,384]{1,0:T(8,128)(2,1)}, bf16[2,3,16,32...) custom-call(bf16[2048,384]{1,0:T(8,128)(2,1)} %get-tuple-element.51., ...), custom_call_target="tpu_custom_call" | custom-call | tf_op jit(solution)/shard_map/middle/pallas_call | solution.py:704
  133.1 133.3 %late.1 = (bf16[2,3,16,32,256]{4,3,2,1,0:T(8,128)(2,1)}, bf16[2,3,16,16,512]{4,3,2,1,0:T(8,128)(2,1)}, bf16[3,3,16,16,512]{4,3,2,1,0:T(8,128)(2,1)}, bf16[1024,768]{1,0:T(8,128)(2,1)}, f32[72,128]{1,0:T(8,128)}) custom-call(bf16[2048,1152]{1,0:T(8,128)(2,1)} %get-tuple-element.50.q_ref.k_ref.v_ref, bf16[2048,384]{1,0:T(8,128)(2,1)} %get-tuple-element.56.go_ref, ...), custom_call_target="tpu_custom_call" | custom-call | tf_op jit(solution)/shard_map/late/pallas_call | solution.py:1064
  266.4 12.1 %finish.1 = (bf16[1024,768]{1,0:T(8,128)(2,1)}, bf16[1024,768]{1,0:T(8,128)(2,1)}, f32[3,16,32,768]{3,2,1,0:T(8,128)}, f32[768,1536]{1,0:T(8,128)}, f32[3,768,38...) custom-call(bf16[1,3,16,32,256]{4,3,2,1,0:T(8,128)(2,1)} %get-tuple-, ...), custom_call_target="tpu_custom_call" | custom-call | tf_op jit(solution)/shard_map/finish/pallas_call | solution.py:1187
